TPU v7x, 512 devices: a whole 4x4x16 slice. The times are simulated.
512 devices in a mesh: dp: 32 (over z_lo, y, core), tensor: 16 (over z_hi, x).
Axes of the slice: x: 4, y: 4, z: 16 (z_hi: 4, z_lo: 4; z = z_hi * 4 + z_lo), core: 2. Of those that a mesh axis runs over, the one named last changes fastest.
Arguments:
- control_in: bfloat16 [4096, 3072], P('dp'), may hold values from -6 to 6
- control_project: bfloat16 [3, 3072, 2048], P(None, 'dp', 'tensor'), may hold values from -1 to 1
- control_output: bfloat16 [3072, 2048], P('dp', 'tensor'), may hold values from -0.5 to 0.5
- query_gain: float32 [128], replicated, may hold values from 0.5 to 8
- key_gain: float32 [128], replicated, may hold values from 0.5 to 8
- base_hidden: bfloat16 [4096, 3072], P('dp'), may hold values from -4 to 4
- base_up: bfloat16 [3072, 6144], P('dp', 'tensor'), may hold values from -0.109375 to 0.109375
- base_down: bfloat16 [3072, 6144], P('dp', 'tensor'), may hold values from -0.078125 to 0.078125
- cotangent: bfloat16 [4096, 3072], P('dp'), may hold values from -6 to 6
Outputs:
- base_out: bfloat16 [4096, 3072], P(('dp', 'tensor'))
- feat_grad: bfloat16 [4096, 3072], P(('dp', 'tensor'))
All inputs are finite; a program needn't handle non-finite values.
Results may differ from a plain program's by a relative error of at most 0.025.
The roundings to bfloat16 on the way count: a program that leaves them out, or rounds other values in their place, can miss the bound.
Values may be sent and summed in bfloat16 or wider, within the bound.
A program may use at most 64 MiB of HBM per device.

v0:
```python
import jax
import jax.numpy as jnp
from jax import lax
from jax.sharding import PartitionSpec as P


def norm_rows(values):
    center = values - jnp.mean(values, axis=-1, keepdims=True)
    spread = jnp.mean(center * center, axis=-1, keepdims=True)
    rstd = lax.rsqrt(spread + 1e-06)
    return (center * rstd, rstd)


def gelu_tanh(values):
    inner = 0.7978845608028654 * (values + 0.044715 * values * values * values)
    return 0.5 * values * (1.0 + jnp.tanh(inner))


def gelu_slope(values):
    inner = 0.7978845608028654 * (values + 0.044715 * values * values * values)
    tangent = jnp.tanh(inner)
    return 0.5 * (1.0 + tangent) + 0.5 * values * (1.0 - tangent * tangent) * 0.7978845608028654 * (
        1.0 + 3.0 * 0.044715 * values * values
    )


def times_transposed(left, right):
    return lax.dot_general(
        left, right, (((1,), (1,)), ((), ())), preferred_element_type=jnp.float32
    )


def head_norm(values, gain):
    square_mean = jnp.mean(values * values, axis=-1, keepdims=True)
    return (values * lax.rsqrt(square_mean + 1e-06) * gain).astype(jnp.bfloat16)


def body(
    control_in,
    control_project,
    control_output,
    query_gain,
    key_gain,
    base_hidden,
    base_up,
    base_down,
    cotangent,
):
    tok_rows = control_in.shape[0]
    head_dim = control_project.shape[2]
    own_rows = tok_rows // lax.axis_size("tensor")
    first_row = lax.axis_index("tensor") * own_rows
    normed_in = norm_rows(control_in.astype(jnp.float32))[0].astype(jnp.bfloat16)
    projected = jnp.einsum(
        "tr,jrc->jtc",
        normed_in,
        lax.all_gather(control_project, "dp", axis=1, tiled=True),
        preferred_element_type=jnp.float32,
    )
    queries = head_norm(projected[0], query_gain)
    keys_own = head_norm(projected[1], key_gain)
    values_own = projected[2].astype(jnp.bfloat16)
    score_scale = 1.0 / head_dim**0.5
    running_max = jnp.full((tok_rows,), -1e30, jnp.float32)
    key_block = lax.all_gather(keys_own, "dp", axis=0, tiled=True)
    value_block = lax.all_gather(values_own, "dp", axis=0, tiled=True)
    scores = times_transposed(queries, key_block) * score_scale
    new_max = jnp.maximum(running_max, jnp.max(scores, axis=1))
    expo = jnp.exp(scores - new_max[:, None])
    running_sum = jnp.sum(expo, axis=1)
    running_acc = jnp.dot(
        expo.astype(jnp.bfloat16), value_block, preferred_element_type=jnp.float32
    )
    mixed = (running_acc / running_sum[:, None]).astype(jnp.bfloat16)
    partial_feat = times_transposed(mixed, lax.all_gather(control_output, "dp", axis=0, tiled=True))
    feat_all = lax.psum(partial_feat.astype(jnp.bfloat16), "tensor").astype(jnp.float32)
    summed = base_hidden.astype(jnp.float32) + feat_all
    nhat, rstd = norm_rows(summed)
    normed = nhat.astype(jnp.bfloat16)
    summed_own = lax.dynamic_slice_in_dim(summed, first_row, own_rows, 0)
    nhat_own = lax.dynamic_slice_in_dim(nhat, first_row, own_rows, 0)
    rstd_own = lax.dynamic_slice_in_dim(rstd, first_row, own_rows, 0)
    up_full = lax.all_gather(base_up, "dp", axis=0, tiled=True)
    pre = jnp.dot(normed, up_full, preferred_element_type=jnp.float32)
    hidden = gelu_tanh(pre).astype(jnp.bfloat16)
    down_full = lax.all_gather(base_down, "dp", axis=0, tiled=True)
    added = lax.psum_scatter(
        times_transposed(hidden, down_full).astype(jnp.bfloat16),
        "tensor",
        scatter_dimension=0,
        tiled=True,
    ).astype(jnp.float32)
    base_out = (summed_own + added).astype(jnp.bfloat16)
    hidden_grad = jnp.dot(cotangent, down_full, preferred_element_type=jnp.float32)
    pre_grad = (hidden_grad * gelu_slope(pre)).astype(jnp.bfloat16)
    normed_grad = lax.psum_scatter(
        times_transposed(pre_grad, up_full).astype(jnp.bfloat16),
        "tensor",
        scatter_dimension=0,
        tiled=True,
    ).astype(jnp.float32)
    cot_own = lax.dynamic_slice_in_dim(cotangent, first_row, own_rows, 0).astype(jnp.float32)
    feat_grad = cot_own + rstd_own * (
        normed_grad
        - jnp.mean(normed_grad, axis=-1, keepdims=True)
        - nhat_own * jnp.mean(normed_grad * nhat_own, axis=-1, keepdims=True)
    )
    return (base_out, feat_grad.astype(jnp.bfloat16))


def solution(mesh):
    placed = (
        P("dp", None),
        P(None, "dp", "tensor"),
        P("dp", "tensor"),
        P(),
        P(),
        P("dp", None),
        P("dp", "tensor"),
        P("dp", "tensor"),
        P("dp", None),
    )
    return jax.shard_map(
        body,
        mesh=mesh,
        in_specs=placed,
        out_specs=(P(("dp", "tensor"), None), P(("dp", "tensor"), None)),
        check_vma=False,
    )
```

profile of v0, /device:TPU:6, one launch (start us, length us, event | category | flops | bytes accessed | tf_op | source)
XLA Modules:
  0.0 799.3 jit_solution(1762166294979302259)
XLA Ops:
  7.2 0.7 all-gather.7.cloned.1.call-update
  8.0 1.3 convert_reduce_fusion
  9.3 1.5 fusion.4
  10.8 69.6 %all-gather.7.cloned.1.call-done = bf16[3,3072,128]{2,1,0:T(8,128)(2,1)} async-done(((bf16[3,96,128]{2,1,0:T(8,128)(2,1)}), bf16[3,3072,128]{2,1,0:T(8,128)(2,1)}) %all-gather.7.cloned.1.call-update) | async-done | bytes 2359312 | tf_op jit(solution)/shard_map/all_gather | solution.py:57
  80.4 2.7 convolution_bitcast_fusion
  83.3 0.7 multiply_convert_fusion.2
  84.0 0.6 slice.28
  84.8 45.9 %all_gather.21 = bf16[3072,128]{1,0:T(8,128)(2,1)} all-gather(bf16[96,128]{1,0:T(8,128)(2,1)S(1)} %copy-done.6), channel_id=1, replica_groups=mesh['dp'=32,'tensor'=16] {'dp'}, dimensions={0}, use_global_device_ids=true | all-gather | bytes 811008 | tf_op jit(solution)/shard_map/all_gather | solution.py:75
  130.7 18.6 %all-gather.9.cloned.1.call-done = bf16[4096,128]{0,1:T(8,128)(2,1)} async-done(((bf16[128,128]{0,1:T(8,128)(2,1)}), bf16[4096,128]{0,1:T(8,128)(2,1)}) %all-gather.9.cloned.1.call-update) | async-done | bytes 1048592 | tf_op jit(solution)/shard_map/all_gather | solution.py:65
  149.3 1.8 fusion.61
  151.6 64.7 %all-gather.15.cloned.1.call-done = bf16[1,4096,128]{1,2,0:T(8,128)(2,1)} async-done(((bf16[1,128,128]{1,2,0:T(8,128)(2,1)}), bf16[1,4096,128]{1,2,0:T(8,128)(2,1)}) %all-gather.15.cloned.1.call-update) | async-done | bytes 1048592 | tf_op jit(solution)/shard_map/all_gather | solution.py:66
  216.3 3.5 convolution_convert_fusion.2
  221.1 203.9 %all-reduce.2.cloned.1.call-done = bf16[128,3072]{1,0:T(8,128)(2,1)} async-done(((bf16[128,3072]{1,0:T(8,128)(2,1)}), bf16[128,3072]{1,0:T(8,128)(2,1)}) %all-reduce.2.cloned.1.call-update) | async-done | bytes 786448 | tf_op jit(solution)/shard_map/psum | solution.py:76
  424.9 2.6 convert_add_fusion
  428.3 66.8 %all-gather.11.cloned.1.call-done = bf16[3072,384]{1,0:T(8,128)(2,1)} async-done(((bf16[96,384]{1,0:T(8,128)(2,1)}), bf16[3072,384]{1,0:T(8,128)(2,1)}) %all-gather.11.cloned.1.call-update) | async-done | bytes 2359312 | tf_op jit(solution)/shard_map/all_gather | solution.py:83
  495.2 2.2 fusion.16
  497.4 64.8 %all-gather.13.cloned.1.call-done = bf16[3072,384]{1,0:T(8,128)(2,1)} async-done(((bf16[96,384]{1,0:T(8,128)(2,1)}), bf16[3072,384]{1,0:T(8,128)(2,1)}) %all-gather.13.cloned.1.call-update) | async-done | bytes 2359312 | tf_op jit(solution)/shard_map/all_gather | solution.py:86
  562.2 4.8 convolution_convert_fusion
  567.1 1.7 convolution_convert_fusion.1
  569.0 108.5 %reduce-scatter.5.cloned.1.call-done = bf16[8,3072]{1,0:T(8,128)(2,1)} async-done(((bf16[128,3072]{1,0:T(8,128)(2,1)}), bf16[8,3072]{1,0:T(8,128)(2,1)}) %reduce-scatter.5.cloned.1.call-update) | async-done | bytes 49168 | tf_op jit(solution)/shard_map/reduce_scatter | solution.py:96
  677.5 1.1 convert_reduce_fusion.1
  678.6 110.7 %reduce-scatter.3.cloned.1.call-done = bf16[8,3072]{1,0:T(8,128)(2,1)} async-done(((bf16[128,3072]{1,0:T(8,128)(2,1)}), bf16[8,3072]{1,0:T(8,128)(2,1)}) %reduce-scatter.3.cloned.1.call-update) | async-done | bytes 49168 | tf_op jit(solution)/shard_map/reduce_scatter | solution.py:87
  789.3 1.6 add_convert_fusion
  790.8 1.6 fusion.37
  (46 shorter events, 2.9 us)
Async XLA Ops:
  7.2 73.3 %copy-start.2 = (bf16[128,3072]{1,0:T(8,128)(2,1)S(1)}, bf16[128,3072]{1,0:T(8,128)(2,1)}, u32[]{:S(2)}) copy-start(bf16[128,3072]{1,0:T(8,128)(2,1)} %param.9) | copy-start | bytes 2359300
  7.2 73.3 %all-gather.7.cloned.1.call-start = ((), (), s32[]{:S(2)}) async-start(), calls=%async_computation.2 | async-start | bytes 2433024 | tf_op jit(solution)/shard_map/all_gather | solution.py:57
  7.9 141.4 %all-gather.9.cloned.1.call-start = ((), (), s32[]{:S(2)}) async-start(), calls=%async_computation.3 | async-start | bytes 1081344 | tf_op jit(solution)/shard_map/all_gather | solution.py:65
  10.8 72.5 %copy-start.7 = (f32[128]{0:T(128)S(1)}, f32[128]{0:T(128)}, u32[]{:S(2)}) copy-start(f32[128]{0:T(128)} %param.13) | copy-start | bytes 1540
  10.8 74.0 %copy-start.6 = (bf16[96,128]{1,0:T(8,128)(2,1)S(1)}, bf16[96,128]{1,0:T(8,128)(2,1)}, u32[]{:S(2)}) copy-start(bf16[96,128]{1,0:T(8,128)(2,1)} %param.11) | copy-start | bytes 73732
  10.8 138.5 %copy-start.8 = (f32[128]{0:T(128)S(1)}, f32[128]{0:T(128)}, u32[]{:S(2)}) copy-start(f32[128]{0:T(128)} %param.12) | copy-start | bytes 1540
  84.0 132.3 %all-gather.15.cloned.1.call-start = ((), (), s32[]{:S(2)}) async-start(), calls=%async_computation.9 | async-start | bytes 1081344 | tf_op jit(solution)/shard_map/all_gather | solution.py:66
  84.7 340.2 %all-reduce.2.cloned.1.call-start = ((), (), s32[]{:S(2)}) async-start(), calls=%async_computation.4 | async-start | bytes 1572864 | tf_op jit(solution)/shard_map/psum | solution.py:76
  151.6 273.4 %copy-start.3 = (bf16[128,3072]{1,0:T(8,128)(2,1)S(1)}, bf16[128,3072]{1,0:T(8,128)(2,1)}, u32[]{:S(2)}) copy-start(bf16[128,3072]{1,0:T(8,128)(2,1)} %param.14) | copy-start | bytes 2359300
  219.8 275.3 %all-gather.11.cloned.1.call-start = ((), (), s32[]{:S(2)}) async-start(), calls=%async_computation.5 | async-start | bytes 2433024 | tf_op jit(solution)/shard_map/all_gather | solution.py:83
  220.4 341.7 %all-gather.13.cloned.1.call-start = ((), (), s32[]{:S(2)}) async-start(), calls=%async_computation.6 | async-start | bytes 2433024 | tf_op jit(solution)/shard_map/all_gather | solution.py:86
  221.0 456.5 %reduce-scatter.5.cloned.1.call-start = ((), (), s32[]{:S(2)}) async-start(), calls=%async_computation.8 | async-start | bytes 835584 | tf_op jit(solution)/shard_map/reduce_scatter | solution.py:96
  424.9 2.6 copy-start.4
  428.3 69.1 %copy-start.1 = (f32[128,3072]{1,0:T(8,128)}, f32[128,3072]{1,0:T(8,128)S(1)}, u32[]{:S(2)}) copy-start(f32[128,3072]{1,0:T(8,128)S(1)} %subtract_multiply_fusion) | copy-start | bytes 4718596
  428.3 133.9 %copy-start.5 = (bf16[128,3072]{1,0:T(8,128)(2,1)S(1)}, bf16[128,3072]{1,0:T(8,128)(2,1)}, u32[]{:S(2)}) copy-start(bf16[128,3072]{1,0:T(8,128)(2,1)} %param.17) | copy-start | bytes 2359300
  562.2 4.9 copy-start
  567.1 222.2 %reduce-scatter.3.cloned.1.call-start = ((), (), s32[]{:S(2)}) async-start(), calls=%async_computation.7 | async-start | bytes 835584 | tf_op jit(solution)/shard_map/reduce_scatter | solution.py:87
Sparse Core Ops, SparseCore 0:
  10.1 70.2 all-gather.6
  84.1 65.1 all-gather.8
  151.9 64.3 all-gather.14
  220.0 204.9 all-reduce.1
  427.1 67.9 all-gather.10
  497.4 64.7 all-gather.12
  567.2 110.2 reduce-scatter.4
  682.1 107.1 reduce-scatter.2
where the time goes:
time: 801 us; the launch traced here: 799 us
  waiting for transfers between devices  709 us (89%)
  blocking collectives  45.9 us (6%)
  matrix products  16.9 us (2%)
  between operations  14.3 us (2%)
  other arithmetic  11.7 us (1%)
    psum x1, waiting for transfers between devices, body(): lax.psum(partial_feat.astype(jnp.bfloat16), 'tensor').astype(jnp.float32)  204 us
    reduce_scatter x1, waiting for transfers between devices, body(): lax.psum_scatter(times_transposed(hidden, down_full).astype(jnp.bfloat16)...  111 us
    reduce_scatter x1, waiting for transfers between devices, body(): lax.psum_scatter(times_transposed(pre_grad, up_full).astype(jnp.bfloat16)...  109 us
    all_gather x1, waiting for transfers between devices, body(): lax.all_gather(control_project, 'dp', axis=1, tiled=True)  69.6 us
    all_gather x1, waiting for transfers between devices, body(): up_full = lax.all_gather(base_up, 'dp', axis=0, tiled=True)  66.8 us
    all_gather x1, waiting for transfers between devices, body(): down_full = lax.all_gather(base_down, 'dp', axis=0, tiled=True)  64.8 us
    all_gather x1, waiting for transfers between devices, body(): value_block = lax.all_gather(values_own, 'dp', axis=0, tiled=True)  64.7 us
    all_gather x1, blocking collectives, body(): lax.all_gather(control_output, 'dp', axis=0, tiled=True)  45.9 us
  transfers between devices with their start and end apart: 8, of which 8 were waited for; matrix products, arithmetic and copies ran while one was open for 2% of the time, Pallas kernels for 0%

commit v1 on v0

v1 whole, which is shorter than its diff:
```python
import functools

import jax
import jax.numpy as jnp
from jax import lax
from jax.experimental import pallas as pl
from jax.experimental.pallas import tpu as pltpu
from jax.sharding import PartitionSpec as P

F32 = jnp.float32
BF16 = jnp.bfloat16
MESH = pl.DeviceIdType.MESH
D = 3072
HALF = D // 2
LANES = HALF // 2


def norm_rows(values):
    center = values - jnp.mean(values, axis=-1, keepdims=True)
    spread = jnp.mean(center * center, axis=-1, keepdims=True)
    rstd = lax.rsqrt(spread + 1e-06)
    return (center * rstd, rstd)


def head_norm(values, gain):
    square_mean = jnp.mean(values * values, axis=-1, keepdims=True)
    return (values * lax.rsqrt(square_mean + 1e-06) * gain).astype(BF16)


def times_transposed(left, right):
    return lax.dot_general(left, right, (((1,), (1,)), ((), ())), preferred_element_type=F32)


def gray(x):
    return x // 2, lax.rem((x + 1) // 2, 2) if not isinstance(x, int) else ((x + 1) // 2) % 2


class Place:
    def __init__(self):
        dp, tensor = lax.axis_index("dp"), lax.axis_index("tensor")
        self.dp, self.tensor = dp, tensor
        self.z, self.y, self.c = dp // 8, lax.rem(dp // 2, 4), lax.rem(dp, 2)
        self.w, self.x = tensor // 4, lax.rem(tensor, 4)
        self.p, self.q = gray(self.x)
        self.u, self.v = gray(self.w)
        flip = lambda i: i + 1 - 2 * lax.rem(i, 2)
        self.flip_q = (dp, self.w * 4 + flip(self.x))
        self.flip_p = (dp, self.w * 4 + 3 - self.x)
        self.flip_v = (dp, flip(self.w) * 4 + self.x)
        self.flip_u = (dp, (3 - self.w) * 4 + self.x)
        self.sibling = self.at(self.z, self.y, 1 - self.c)

    def at(self, z, y, c):
        return (z * 8 + y * 2 + c, self.tensor)

    def zs(self, j):
        return lax.rem(self.z + (j + 4), 4)

    def ys(self, j):
        return lax.rem(self.y + (j + 4), 4)

    def partners(self):
        return [self.at(self.zs(j), self.y, self.c) for j in (1, 2, 3)] + [
            self.at(self.z, self.ys(1), self.c),
            self.at(self.z, self.ys(-1), self.c),
            self.sibling,
            self.flip_q,
            self.flip_p,
            self.flip_v,
            self.flip_u,
        ]


def remote(src, dst, send, recv, device):
    return pltpu.make_async_remote_copy(
        src_ref=src, dst_ref=dst, send_sem=send, recv_sem=recv, device_id=device, device_id_type=MESH
    )


class Gather:
    def __init__(self, at, buf, send, recv):
        self.at, self.buf, self.send, self.recv = at, buf, send, recv

    def slot(self, z, y, c):
        return self.buf.at[z, y * 2 + c]

    def line(self, y, c):
        return self.buf.at[:, y * 2 + c]

    def copy(self, ref, group, sem, device):
        return remote(ref, ref, self.send.at[group], self.recv.at[sem], device)

    def wait(self, ref, sem):
        self.copy(ref, 0, sem, self.at.sibling).wait_recv()

    def both_ways(self, j):
        at = self.at
        ref = self.slot(at.zs(-j), at.y, at.c)
        self.copy(ref, 1, 3 + j, at.at(at.z, at.ys(1), at.c)).start()
        self.copy(ref, 1, 7 + j, at.at(at.z, at.ys(-1), at.c)).start()

    def start(self):
        at = self.at
        for j in (1, 2, 3):
            self.copy(self.slot(at.z, at.y, at.c), 0, j - 1, at.at(at.zs(j), at.y, at.c)).start()
        self.both_ways(0)

    def middle(self):
        at = self.at
        for j in (1, 3, 2):
            self.wait(self.slot(at.zs(-j), at.y, at.c), j - 1)
            self.both_ways(j)
        self.copy(self.line(at.y, at.c), 3, 15, at.sibling).start()

    def relay(self):
        at = self.at
        for j in (0, 1, 3, 2):
            below, above = self.slot(at.zs(-j), at.ys(-1), at.c), self.slot(at.zs(-j), at.ys(1), at.c)
            self.wait(below, 3 + j)
            if j in (0, 3):
                self.copy(below, 2, 11 + j, at.at(at.z, at.ys(1), at.c)).start()
            self.wait(above, 7 + j)
            if j in (1, 2):
                self.copy(above, 2, 11 + j, at.at(at.z, at.ys(-1), at.c)).start()
        self.copy(self.line(at.ys(-1), at.c), 3, 16, at.sibling).start()
        self.copy(self.line(at.ys(1), at.c), 3, 17, at.sibling).start()

    def finish(self):
        at = self.at
        for j in (0, 1, 3, 2):
            self.wait(self.slot(at.zs(-j), at.ys(2), at.c), 11 + j)
        self.copy(self.line(at.ys(2), at.c), 3, 18, at.sibling).start()
        for sem, step in ((15, 0), (16, -1), (17, 1), (18, 2)):
            self.wait(self.line(at.ys(step), 1 - at.c), sem)

    def drain(self):
        for group, ref in enumerate((self.buf.at[0:3, 0], self.buf.at[:, 0:2], self.buf.at[:, 0], self.buf.at[:, 0:4])):
            self.copy(ref, group, 0, self.at.sibling).wait_send()


def lanes(h):
    return pl.ds(h * LANES, LANES)


class Scatter:
    def __init__(self, at, part, r1, s1, r2, t32, t16, r3, s3, r4, send, recv):
        self.at, self.part, self.r1, self.s1, self.r2 = at, part, r1, s1, r2
        self.t32, self.t16, self.r3, self.s3, self.r4 = t32, t16, r3, s3, r4
        self.send, self.recv = send, recv

    def copies(self, level):
        at, part = self.at, self.part
        if level == 0:
            pairs = (
                (part.at[:, 1 - at.q, :, :, :, lanes(0)], self.r1.at[0], at.flip_q),
                (part.at[1 - at.p, :, :, :, :, lanes(1)], self.r1.at[1], at.flip_p),
            )
        elif level == 1:
            pairs = ((self.s1.at[0], self.r2.at[0], at.flip_p), (self.s1.at[1], self.r2.at[1], at.flip_q))
        elif level == 2:
            pairs = (
                (self.t16.at[0, :, 1 - at.v], self.r3.at[0], at.flip_v),
                (self.t16.at[1, 1 - at.u], self.r3.at[1], at.flip_u),
            )
        else:
            pairs = ((self.s3.at[0], self.r4.at[0], at.flip_u), (self.s3.at[1], self.r4.at[1], at.flip_v))
        return [
            remote(src, dst, self.send.at[2 * level + h], self.recv.at[2 * level + h], device)
            for h, (src, dst, device) in enumerate(pairs)
        ]

    def x1(self):
        for copy in self.copies(0):
            copy.start()

    def x2(self):
        at = self.at
        arrive, leave = self.copies(0), self.copies(1)
        for h, (p, q, keep) in enumerate(((1 - at.p, at.q, 1 - at.p), (at.p, 1 - at.q, 1 - at.q))):
            arrive[h].wait_recv()
            mine = self.part[p, q, :, :, :, h * LANES : (h + 1) * LANES].astype(F32)
            self.s1[h] = (mine + self.r1[h, keep].astype(F32)).astype(BF16)
            leave[h].start()

    def z1(self):
        at = self.at
        arrive, leave = self.copies(1), self.copies(2)
        for h, keep in enumerate((at.p, at.q)):
            arrive[h].wait_recv()
            mine = self.part[at.p, at.q, :, :, :, h * LANES : (h + 1) * LANES].astype(F32)
            total = mine + self.r1[h, keep].astype(F32) + self.r2[h].astype(F32)
            self.t32[h] = total
            self.t16[h] = total.astype(BF16)
            leave[h].start()

    def z2(self):
        at = self.at
        arrive, leave = self.copies(2), self.copies(3)
        for h, (u, v, keep) in enumerate(((1 - at.u, at.v, 1 - at.u), (at.u, 1 - at.v, 1 - at.v))):
            arrive[h].wait_recv()
            self.s3[h] = (self.t32[h, u, v] + self.r3[h, keep].astype(F32)).astype(BF16)
            leave[h].start()

    def done(self):
        at = self.at
        arrive = self.copies(3)
        halves = []
        for h, keep in enumerate((at.u, at.v)):
            arrive[h].wait_recv()
            halves.append(self.t32[h, at.u, at.v] + self.r3[h, keep].astype(F32) + self.r4[h].astype(F32))
        both = jnp.concatenate(halves, axis=1)
        return jnp.concatenate([both[0:8], both[8:16]], axis=1)

    def drain(self):
        for level in range(4):
            for copy in self.copies(level):
                copy.wait_send()

    def fill(self, left, matrix):
        for n in range(4):
            z, k = n // 2, 4 * (n % 2)
            depth = matrix.shape[3]
            low = times_transposed(left, matrix[z, k : k + 4].reshape(384, depth))
            high = times_transposed(left, matrix[z + 2, k : k + 4].reshape(384, depth))
            both = jnp.concatenate([low.reshape(16, 8, 384), high.reshape(16, 8, 384)], axis=1).astype(BF16)
            for t in range(16):
                (u, v), (p, q) = gray(t // 4), gray(t % 4)
                self.part[p, q, u, v, :, n * 384 : (n + 1) * 384] = both[t]


class Spread:
    def __init__(self, at, buf, send, recv):
        self.at, self.buf, self.send, self.recv = at, buf, send, recv

    def refs(self, level, h, mirror):
        at, buf = self.at, self.buf
        p, q, u, v = at.p, at.q, at.u, at.v
        everything = slice(None)
        if level == 0:
            if mirror:
                u, v = (u, 1 - v) if h == 0 else (1 - u, v)
            return buf.at[p, q, u, v, :, lanes(h)]
        if level == 1:
            if h == 0:
                return buf.at[p, q, 1 - u if mirror else u, :, :, lanes(h)]
            return buf.at[p, q, :, 1 - v if mirror else v, :, lanes(h)]
        if level == 2:
            if mirror:
                p, q = (p, 1 - q) if h == 0 else (1 - p, q)
            return buf.at[p, q, :, :, :, lanes(h)]
        if h == 0:
            return buf.at[1 - p if mirror else p, :, :, :, :, lanes(h)]
        return buf.at[:, 1 - q if mirror else q, :, :, :, lanes(h)]

    def copy(self, level, h, mirror=False):
        at = self.at
        device = ((at.flip_v, at.flip_u), (at.flip_u, at.flip_v), (at.flip_q, at.flip_p), (at.flip_p, at.flip_q))[level][h]
        ref = self.refs(level, h, mirror)
        return remote(ref, ref, self.send.at[2 * level + h], self.recv.at[2 * level + h], device)

    def step(self, level):
        for h in range(2):
            if level:
                self.copy(level - 1, h, True).wait_recv()
            if level < 4:
                self.copy(level, h).start()

    def drain(self):
        for level in range(4):
            for h in range(2):
                self.copy(level, h).wait_send()


def own_rows(ref, tensor):
    pair = ref[pl.ds(pl.multiple_of((tensor // 2) * 16, 16), 16), :].astype(F32)
    return jnp.where(lax.rem(tensor, 2) == 0, pair[0:8], pair[8:16])


def kernel(
    control_in, control_project, control_output, query_gain, key_gain, base_hidden, base_up, base_down, cotangent,
    base_out, feat_grad,
    wp_buf, kv_buf, co_buf, up_buf, down_buf, normed_in, scores, weights, spread_buf, normed, hidden_grad,
    part, r1, s1, r2, t32, t16, r3, s3, r4,
    gather_send, gather_recv, scatter_send, scatter_recv, spread_send, spread_recv,
):
    at = Place()
    barrier = pltpu.get_barrier_semaphore()
    partners = at.partners()
    for device in partners:
        pl.semaphore_signal(barrier, inc=1, device_id=device, device_id_type=MESH)

    wp, kv, co, up, down = (
        Gather(at, buf, gather_send.at[i], gather_recv.at[i])
        for i, buf in enumerate((wp_buf, kv_buf, co_buf, up_buf, down_buf))
    )
    feat, added, grad = (
        Scatter(at, *(ref.at[i] for ref in (part, r1, s1, r2, t32, t16, r3, s3, r4, scatter_send, scatter_recv)))
        for i in range(3)
    )
    spread = Spread(at, spread_buf, spread_send, spread_recv)

    yc = at.y * 2 + at.c
    for j in range(3):
        wp_buf[at.z, yc, :, j * 128 : (j + 1) * 128] = control_project[j]
    co_buf[at.z, yc] = control_output[...]
    up_buf[at.z, yc] = base_up[...]
    down_buf[at.z, yc] = base_down[...]
    pl.semaphore_wait(barrier, len(partners))

    wp.start()
    normed_in[...] = norm_rows(control_in[...].astype(F32))[0].astype(BF16)
    wp.middle()
    co.start()
    wp.relay()
    co.middle()
    wp.finish()
    projected = jnp.dot(normed_in[...], wp_buf[...].reshape(D, 384), preferred_element_type=F32)
    queries = head_norm(projected[:, 0:128], query_gain[...])
    kv_buf[at.z, yc, :, 0:128] = head_norm(projected[:, 128:256], key_gain[...])
    kv_buf[at.z, yc, :, 128:256] = projected[:, 256:384].astype(BF16)
    kv.start()
    co.relay()
    kv.middle()
    co.finish()
    kv.relay()
    up.start()
    kv.finish()
    down.start()
    for z in range(4):
        block = kv_buf[z].reshape(1024, 256)
        scores[:, z * 1024 : (z + 1) * 1024] = times_transposed(queries, block[:, 0:128]) * (1.0 / 128**0.5)
    up.middle()
    totals = []
    for r in range(4):
        rows = slice(r * 32, (r + 1) * 32)
        block = scores[rows, :]
        expo = jnp.exp(block - jnp.max(block, axis=1, keepdims=True))
        totals.append(jnp.sum(expo, axis=1, keepdims=True))
        weights[rows, :] = expo.astype(BF16)
    total = jnp.concatenate(totals, axis=0)
    accum = jnp.zeros((128, 128), F32)
    for z in range(4):
        accum = accum + jnp.dot(
            weights[:, z * 1024 : (z + 1) * 1024],
            kv_buf[z].reshape(1024, 256)[:, 128:256],
            preferred_element_type=F32,
        )
    mixed = (accum / total).astype(BF16)
    feat.fill(mixed, co_buf)
    feat.x1()
    up.relay()
    down.middle()
    feat.x2()
    feat.z1()
    up.finish()
    down.relay()
    feat.z2()
    down.finish()
    hidden_grad[...] = jnp.dot(cotangent[...], down_buf[...].reshape(D, 384), preferred_element_type=F32)
    summed = own_rows(base_hidden, at.tensor) + feat.done()
    nhat, rstd = norm_rows(summed)
    spread_buf[at.p, at.q, at.u, at.v] = jnp.concatenate([nhat[:, :HALF], nhat[:, HALF:]], axis=0).astype(BF16)
    for level in range(5):
        spread.step(level)
    for k in range(8):
        pair = []
        for t in (2 * k, 2 * k + 1):
            (u, v), (p, q) = gray(t // 4), gray(t % 4)
            pair.append(spread_buf[p, q, u, v].astype(F32))
        for h in range(2):
            normed[k * 16 : (k + 1) * 16, h * HALF : (h + 1) * HALF] = jnp.concatenate(
                [block[h * 8 : (h + 1) * 8] for block in pair], axis=0
            ).astype(BF16)
    pre = jnp.dot(normed[...], up_buf[...].reshape(D, 384), preferred_element_type=F32)
    tangent = jnp.tanh(0.7978845608028654 * (pre + 0.044715 * pre * pre * pre))
    hidden = (0.5 * pre * (1.0 + tangent)).astype(BF16)
    slope = 0.5 * (1.0 + tangent) + 0.5 * pre * (1.0 - tangent * tangent) * 0.7978845608028654 * (
        1.0 + 3.0 * 0.044715 * pre * pre
    )
    pre_grad = (hidden_grad[...] * slope).astype(BF16)
    added.fill(hidden, down_buf)
    added.x1()
    grad.fill(pre_grad, up_buf)
    grad.x1()
    added.x2()
    grad.x2()
    added.z1()
    grad.z1()
    added.z2()
    grad.z2()
    base_out[...] = summed + added.done()
    normed_grad = grad.done()
    feat_grad[...] = own_rows(cotangent, at.tensor) + rstd * (
        normed_grad
        - jnp.mean(normed_grad, axis=-1, keepdims=True)
        - nhat * jnp.mean(normed_grad * nhat, axis=-1, keepdims=True)
    )
    for each in (wp, kv, co, up, down, feat, added, grad, spread):
        each.drain()


def body(*args):
    args = list(args)
    args[3] = args[3].reshape(1, 128)
    args[4] = args[4].reshape(1, 128)
    vmem = pl.BlockSpec(memory_space=pltpu.VMEM)
    out = pl.pallas_call(
        kernel,
        out_shape=[jax.ShapeDtypeStruct((8, D), F32)] * 2,
        in_specs=[vmem] * 9,
        out_specs=[vmem] * 2,
        scratch_shapes=[
            pltpu.VMEM((4, 8, 96, 384), BF16),
            pltpu.VMEM((4, 8, 128, 256), BF16),
            pltpu.VMEM((4, 8, 96, 128), BF16),
            pltpu.VMEM((4, 8, 96, 384), BF16),
            pltpu.VMEM((4, 8, 96, 384), BF16),
            pltpu.VMEM((128, D), BF16),
            pltpu.VMEM((128, 4096), F32),
            pltpu.VMEM((128, 4096), BF16),
            pltpu.VMEM((2, 2, 2, 2, 16, HALF), BF16),
            pltpu.VMEM((128, D), BF16),
            pltpu.VMEM((128, 384), F32),
            pltpu.VMEM((3, 2, 2, 2, 2, 16, HALF), BF16),
            pltpu.VMEM((3, 2, 2, 2, 2, 16, LANES), BF16),
            pltpu.VMEM((3, 2, 2, 2, 16, LANES), BF16),
            pltpu.VMEM((3, 2, 2, 2, 16, LANES), BF16),
            pltpu.VMEM((3, 2, 2, 2, 16, LANES), F32),
            pltpu.VMEM((3, 2, 2, 2, 16, LANES), BF16),
            pltpu.VMEM((3, 2, 2, 16, LANES), BF16),
            pltpu.VMEM((3, 2, 16, LANES), BF16),
            pltpu.VMEM((3, 2, 16, LANES), BF16),
            pltpu.SemaphoreType.DMA((5, 4)),
            pltpu.SemaphoreType.DMA((5, 19)),
            pltpu.SemaphoreType.DMA((3, 8)),
            pltpu.SemaphoreType.DMA((3, 8)),
            pltpu.SemaphoreType.DMA((8,)),
            pltpu.SemaphoreType.DMA((8,)),
        ],
        compiler_params=pltpu.CompilerParams(
            collective_id=0, has_side_effects=True, vmem_limit_bytes=50 * 1024 * 1024
        ),
    )(*args)
    return tuple(each.astype(BF16) for each in out)


def solution(mesh):
    placed = (
        P("dp", None),
        P(None, "dp", "tensor"),
        P("dp", "tensor"),
        P(),
        P(),
        P("dp", None),
        P("dp", "tensor"),
        P("dp", "tensor"),
        P("dp", None),
    )
    return jax.shard_map(
        body,
        mesh=mesh,
        in_specs=placed,
        out_specs=(P(("dp", "tensor"), None), P(("dp", "tensor"), None)),
        check_vma=False,
    )
```

time: 801 us -> 137 us (0.17)
  the two profiles are of different devices: /device:TPU:6 before, /device:TPU:32 now
where the time goes in v1:
time: 137 us
  Pallas kernels  127 us (93%)
  local copies, waits for them, and re-layouts  7.44 us (5%)
    pallas_call x1, Pallas kernels, body(): pl.pallas_call(kernel, out_shape=[jax.ShapeDtypeStruct((8, D), F32)] * 2,...  127 us
    unnamed x18, local copies, waits for them, and re-layouts  7.44 us

profile of v1, /device:TPU:32, one launch (start us, length us, event | category | flops | bytes accessed | tf_op | source)
XLA Modules:
  0.0 136.7 jit_solution(7448207895191019072)
XLA Ops:
  0.6 0.0 copy-start.7
  0.6 0.0 copy-start.8
  0.7 0.6 copy-done.7
  1.3 0.0 copy-done.8
  1.3 0.0 copy-start
  1.3 1.1 copy-done
  2.4 0.0 copy-start.1
  2.4 1.1 copy-done.1
  3.6 0.0 copy-start.2
  3.6 1.1 copy-done.2
  4.7 0.0 copy-start.3
  4.7 0.9 copy-done.3
  5.6 0.0 copy-start.4
  5.6 0.9 copy-done.4
  6.5 0.0 copy-start.5
  6.5 0.9 copy-done.5
  7.4 0.0 copy-start.6
  7.4 0.7 copy-done.6
  8.1 127.4 %shard_map.104 = (f32[8,3072]{1,0:T(8,128)S(1)}, f32[8,3072]{1,0:T(8,128)S(1)}) custom-call(bf16[128,3072]{1,0:T(8,128)(2,1)S(1)} %copy-done, bf16[3,96,128]{2,1,0:T(8,128)(2,1)S(1)} %copy-done.3, bf16[96,128]{1,0:T(8,128)(2,1)S(1)} %copy-done.6, f32[1,128]{1,0:T(1,128)S(1)} %bitcast.2, f32[1,128]{1,0:T(1,128)S(1)} %bitcast.3, ...), custom_call_target="tpu_custom_call" | custom-call | tf_op jit(solution)/shard_map/pallas_call | solution.py:407
  135.5 0.6 convert_element_type.6
  136.1 0.6 convert_element_type.7
Async XLA Ops:
  0.6 0.7 copy-start.7
  0.6 0.7 copy-start.8
  1.3 1.1 copy-start
  2.4 1.1 copy-start.1
  3.6 1.1 copy-start.2
  4.7 0.9 copy-start.3
  5.6 0.9 copy-start.4
  6.5 0.9 copy-start.5
  7.4 0.7 copy-start.6

commit v2 on v1

--- a/solution.py
+++ b/solution.py
@@ -59,16 +59,29 @@
     def ys(self, j):
         return lax.rem(self.y + (j + 4), 4)
 
+    def xs(self, j):
+        return lax.rem(self.x + (j + 4), 4)
+
+    def ws(self, j):
+        return lax.rem(self.w + (j + 4), 4)
+
+    def tensor_at(self, w, x):
+        return (self.dp, w * 4 + x)
+
     def partners(self):
-        return [self.at(self.zs(j), self.y, self.c) for j in (1, 2, 3)] + [
-            self.at(self.z, self.ys(1), self.c),
-            self.at(self.z, self.ys(-1), self.c),
-            self.sibling,
-            self.flip_q,
-            self.flip_p,
-            self.flip_v,
-            self.flip_u,
-        ]
+        return (
+            [self.at(self.zs(j), self.y, self.c) for j in (1, 2, 3)]
+            + [self.at(self.z, self.ys(j), self.c) for j in (1, -1)]
+            + [self.sibling]
+            + self.x_peers()
+            + self.w_peers()
+        )
+
+    def x_peers(self):
+        return [self.tensor_at(self.w, self.xs(j)) for j in (1, 2, 3)]
+
+    def w_peers(self):
+        return [self.tensor_at(self.ws(j), self.x) for j in (1, 2, 3)]
 
 
 def remote(src, dst, send, recv, device):
@@ -82,10 +95,10 @@
         self.at, self.buf, self.send, self.recv = at, buf, send, recv
 
     def slot(self, z, y, c):
-        return self.buf.at[z, y * 2 + c]
+        return self.buf.at[z, y, c]
 
     def line(self, y, c):
-        return self.buf.at[:, y * 2 + c]
+        return self.buf.at[:, y, c]
 
     def copy(self, ref, group, sem, device):
         return remote(ref, ref, self.send.at[group], self.recv.at[sem], device)
@@ -101,7 +114,7 @@
 
     def start(self):
         at = self.at
-        for j in (1, 2, 3):
+        for j in (1, 3, 2):
             self.copy(self.slot(at.z, at.y, at.c), 0, j - 1, at.at(at.zs(j), at.y, at.c)).start()
         self.both_ways(0)
 
@@ -130,12 +143,49 @@
         for j in (0, 1, 3, 2):
             self.wait(self.slot(at.zs(-j), at.ys(2), at.c), 11 + j)
         self.copy(self.line(at.ys(2), at.c), 3, 18, at.sibling).start()
+
+    def settle(self):
+        at = self.at
         for sem, step in ((15, 0), (16, -1), (17, 1), (18, 2)):
             self.wait(self.line(at.ys(step), 1 - at.c), sem)
 
     def drain(self):
-        for group, ref in enumerate((self.buf.at[0:3, 0], self.buf.at[:, 0:2], self.buf.at[:, 0], self.buf.at[:, 0:4])):
+        buf = self.buf
+        for group, ref in enumerate((buf.at[0:3, 0, 0], buf.at[:, 0], buf.at[:, 0, 0], buf.at[:, :, 0])):
             self.copy(ref, group, 0, self.at.sibling).wait_send()
+
+
+class Across:
+    def __init__(self, at, buf, send, recv):
+        self.at, self.buf, self.send, self.recv = at, buf, send, recv
+
+    def line(self, x, step):
+        return self.buf.at[x, :, self.at.ys(step), self.at.c]
+
+    def copy(self, ref, group, sem, device):
+        return remote(ref, ref, self.send.at[group], self.recv.at[sem], device)
+
+    def start(self, *steps):
+        at = self.at
+        for step in steps:
+            for i in (1, 3, 2):
+                self.copy(self.line(at.x, step), 0, (step + 1) * 3 + i - 1, at.tensor_at(at.w, at.xs(i))).start()
+
+    def swap(self):
+        at = self.at
+        for i in (1, 3, 2):
+            for step in (0, -1, 1, 2):
+                self.copy(self.line(at.xs(-i), step), 0, (step + 1) * 3 + i - 1, at.sibling).wait_recv()
+            self.copy(self.buf.at[at.xs(-i), :, :, at.c], 1, 12 + i - 1, at.sibling).start()
+
+    def settle(self):
+        at = self.at
+        for i in (1, 3, 2):
+            self.copy(self.buf.at[at.xs(-i), :, :, 1 - at.c], 1, 12 + i - 1, at.sibling).wait_recv()
+
+    def drain(self):
+        for group in range(2):
+            self.copy(self.buf.at[0:3, :, :, 0], group, 0, self.at.sibling).wait_send()
 
 
 def lanes(h):
@@ -218,70 +268,76 @@
 
     def fill(self, left, matrix):
         for n in range(4):
-            z, k = n // 2, 4 * (n % 2)
-            depth = matrix.shape[3]
-            low = times_transposed(left, matrix[z, k : k + 4].reshape(384, depth))
-            high = times_transposed(left, matrix[z + 2, k : k + 4].reshape(384, depth))
+            low = times_transposed(left, row_block(matrix, n))
+            high = times_transposed(left, row_block(matrix, n + 4))
             both = jnp.concatenate([low.reshape(16, 8, 384), high.reshape(16, 8, 384)], axis=1).astype(BF16)
             for t in range(16):
                 (u, v), (p, q) = gray(t // 4), gray(t % 4)
                 self.part[p, q, u, v, :, n * 384 : (n + 1) * 384] = both[t]
 
 
+class Direct:
+    def __init__(self, send, recv, peers):
+        self.send, self.recv, self.peers = send, recv, peers
+
+    def copy(self, j, src, dst):
+        return remote(src, dst, self.send.at[j - 1], self.recv.at[j - 1], self.peers[j - 1])
+
+
 class Spread:
     def __init__(self, at, buf, send, recv):
         self.at, self.buf, self.send, self.recv = at, buf, send, recv
 
-    def refs(self, level, h, mirror):
-        at, buf = self.at, self.buf
-        p, q, u, v = at.p, at.q, at.u, at.v
-        everything = slice(None)
-        if level == 0:
-            if mirror:
-                u, v = (u, 1 - v) if h == 0 else (1 - u, v)
-            return buf.at[p, q, u, v, :, lanes(h)]
-        if level == 1:
-            if h == 0:
-                return buf.at[p, q, 1 - u if mirror else u, :, :, lanes(h)]
-            return buf.at[p, q, :, 1 - v if mirror else v, :, lanes(h)]
-        if level == 2:
-            if mirror:
-                p, q = (p, 1 - q) if h == 0 else (1 - p, q)
-            return buf.at[p, q, :, :, :, lanes(h)]
-        if h == 0:
-            return buf.at[1 - p if mirror else p, :, :, :, :, lanes(h)]
-        return buf.at[:, 1 - q if mirror else q, :, :, :, lanes(h)]
-
-    def copy(self, level, h, mirror=False):
-        at = self.at
-        device = ((at.flip_v, at.flip_u), (at.flip_u, at.flip_v), (at.flip_q, at.flip_p), (at.flip_p, at.flip_q))[level][h]
-        ref = self.refs(level, h, mirror)
-        return remote(ref, ref, self.send.at[2 * level + h], self.recv.at[2 * level + h], device)
-
-    def step(self, level):
-        for h in range(2):
-            if level:
-                self.copy(level - 1, h, True).wait_recv()
-            if level < 4:
-                self.copy(level, h).start()
+    def copy(self, ref, group, sem, device):
+        return remote(ref, ref, self.send.at[group], self.recv.at[sem], device)
+
+    def along_x(self, j):
+        at = self.at
+        for i in (1, 3, 2):
+            self.copy(self.buf.at[at.ws(-j), at.x], 1, 3 + 3 * j + i - 1, at.tensor_at(at.w, at.xs(i))).start()
+
+    def start(self):
+        at = self.at
+        for j in (2, 1, 3):
+            self.copy(self.buf.at[at.w, at.x], 0, j - 1, at.tensor_at(at.ws(j), at.x)).start()
+        self.along_x(0)
+
+    def finish(self):
+        at = self.at
+        for j in (1, 3, 2):
+            self.copy(self.buf.at[at.ws(-j), at.x], 0, j - 1, at.sibling).wait_recv()
+            self.along_x(j)
+        for j in (0, 1, 3, 2):
+            for i in (1, 3, 2):
+                self.copy(self.buf.at[at.ws(-j), at.xs(-i)], 1, 3 + 3 * j + i - 1, at.sibling).wait_recv()
 
     def drain(self):
-        for level in range(4):
-            for h in range(2):
-                self.copy(level, h).wait_send()
-
-
-def own_rows(ref, tensor):
-    pair = ref[pl.ds(pl.multiple_of((tensor // 2) * 16, 16), 16), :].astype(F32)
+        self.copy(self.buf.at[0:3, 0], 0, 0, self.at.sibling).wait_send()
+        self.copy(self.buf.at[0:3], 1, 0, self.at.sibling).wait_send()
+
+
+def row_block(matrix, n):
+    y = 2 * (n % 2)
+    return matrix[n // 2, y : y + 2].reshape(384, matrix.shape[-1])
+
+
+def row_pair(ref, tensor):
+    return ref.at[pl.ds(pl.multiple_of((tensor // 2) * 16, 16), 16), :]
+
+
+def own_rows(pair, tensor):
+    pair = pair.astype(F32)
     return jnp.where(lax.rem(tensor, 2) == 0, pair[0:8], pair[8:16])
 
 
 def kernel(
     control_in, control_project, control_output, query_gain, key_gain, base_hidden, base_up, base_down, cotangent,
     base_out, feat_grad,
-    wp_buf, kv_buf, co_buf, up_buf, down_buf, normed_in, scores, weights, spread_buf, normed, hidden_grad,
+    w_buf, k_buf, v_buf, co_buf, up_buf, down_buf, own_in, own_gain, own_base, own_cot,
+    normed_in, scores, weights, mix_send, mix_recv, feat32, feat16, feat_recv, spread_buf, normed, hidden_grad,
     part, r1, s1, r2, t32, t16, r3, s3, r4,
-    gather_send, gather_recv, scatter_send, scatter_recv, spread_send, spread_recv,
+    local_sem, gather_send, gather_recv, across_send, across_recv, direct_send, direct_recv,
+    scatter_send, scatter_recv, spread_send, spread_recv,
 ):
     at = Place()
     barrier = pltpu.get_barrier_semaphore()
@@ -289,47 +345,96 @@
     for device in partners:
         pl.semaphore_signal(barrier, inc=1, device_id=device, device_id_type=MESH)
 
-    wp, kv, co, up, down = (
+    wq, wk, wv, ks, vs, co, up, down = (
         Gather(at, buf, gather_send.at[i], gather_recv.at[i])
-        for i, buf in enumerate((wp_buf, kv_buf, co_buf, up_buf, down_buf))
-    )
-    feat, added, grad = (
+        for i, buf in enumerate(
+            (w_buf.at[0], w_buf.at[1], w_buf.at[2], k_buf, v_buf, co_buf.at[at.x], up_buf, down_buf)
+        )
+    )
+    co_x = Across(at, co_buf, across_send, across_recv)
+    added, grad = (
         Scatter(at, *(ref.at[i] for ref in (part, r1, s1, r2, t32, t16, r3, s3, r4, scatter_send, scatter_recv)))
-        for i in range(3)
+        for i in range(2)
     )
     spread = Spread(at, spread_buf, spread_send, spread_recv)
-
-    yc = at.y * 2 + at.c
-    for j in range(3):
-        wp_buf[at.z, yc, :, j * 128 : (j + 1) * 128] = control_project[j]
-    co_buf[at.z, yc] = control_output[...]
-    up_buf[at.z, yc] = base_up[...]
-    down_buf[at.z, yc] = base_down[...]
+    heads = Direct(direct_send.at[0], direct_recv.at[0], at.x_peers())
+    feats = Direct(direct_send.at[1], direct_recv.at[1], at.w_peers())
+
+    def own(gather):
+        return gather.slot(at.z, at.y, at.c)
+
+    loads = [
+        pltpu.make_async_copy(src, dst, local_sem.at[i])
+        for i, (src, dst) in enumerate(
+            (
+                (control_project.at[1], own(wk)),
+                (control_project.at[2], own(wv)),
+                (control_project.at[0], own(wq)),
+                (control_in, own_in),
+                (control_output, own(co)),
+                (query_gain, own_gain.at[0]),
+                (key_gain, own_gain.at[1]),
+                (base_up, own(up)),
+                (base_down, own(down)),
+                (row_pair(base_hidden, at.tensor), own_base),
+                (cotangent, own_cot),
+            )
+        )
+    ]
+    for load in loads:
+        load.start()
     pl.semaphore_wait(barrier, len(partners))
 
-    wp.start()
-    normed_in[...] = norm_rows(control_in[...].astype(F32))[0].astype(BF16)
-    wp.middle()
+    for load, gather in zip(loads, (wk, wv, wq)):
+        load.wait()
+        gather.start()
+    loads[3].wait()
+    normed_in[...] = norm_rows(own_in[...].astype(F32))[0].astype(BF16)
+    loads[4].wait()
+    wk.middle()
+    wv.middle()
+    wq.middle()
     co.start()
-    wp.relay()
+    wk.relay()
+    wv.relay()
+    wk.finish()
+    wq.relay()
+    wv.finish()
     co.middle()
-    wp.finish()
-    projected = jnp.dot(normed_in[...], wp_buf[...].reshape(D, 384), preferred_element_type=F32)
-    queries = head_norm(projected[:, 0:128], query_gain[...])
-    kv_buf[at.z, yc, :, 0:128] = head_norm(projected[:, 128:256], key_gain[...])
-    kv_buf[at.z, yc, :, 128:256] = projected[:, 256:384].astype(BF16)
-    kv.start()
+    co_x.start(0)
+    for load in loads[5:]:
+        load.wait()
+    wk.settle()
+    keys = jnp.dot(normed_in[...], w_buf[1].reshape(D, 128), preferred_element_type=F32)
+    k_buf[at.z, at.y, at.c] = head_norm(keys, own_gain[1])
+    ks.start()
+    wv.settle()
+    values = jnp.dot(normed_in[...], w_buf[2].reshape(D, 128), preferred_element_type=F32)
+    v_buf[at.z, at.y, at.c] = values.astype(BF16)
+    vs.start()
+    wq.finish()
     co.relay()
-    kv.middle()
+    co_x.start(-1, 1)
+    ks.middle()
+    wq.settle()
+    queries = head_norm(
+        jnp.dot(normed_in[...], w_buf[0].reshape(D, 128), preferred_element_type=F32), own_gain[0]
+    )
+    vs.middle()
     co.finish()
-    kv.relay()
+    co_x.start(2)
+    ks.relay()
+    vs.relay()
     up.start()
-    kv.finish()
+    ks.finish()
+    vs.finish()
     down.start()
+    co.settle()
+    ks.settle()
     for z in range(4):
-        block = kv_buf[z].reshape(1024, 256)
-        scores[:, z * 1024 : (z + 1) * 1024] = times_transposed(queries, block[:, 0:128]) * (1.0 / 128**0.5)
-    up.middle()
+        block = k_buf[z].reshape(1024, 128)
+        scores[:, z * 1024 : (z + 1) * 1024] = times_transposed(queries, block) * (1.0 / 128**0.5)
+    co_x.swap()
     totals = []
     for r in range(4):
         rows = slice(r * 32, (r + 1) * 32)
@@ -338,35 +443,54 @@
         totals.append(jnp.sum(expo, axis=1, keepdims=True))
         weights[rows, :] = expo.astype(BF16)
     total = jnp.concatenate(totals, axis=0)
+    vs.settle()
     accum = jnp.zeros((128, 128), F32)
     for z in range(4):
         accum = accum + jnp.dot(
-            weights[:, z * 1024 : (z + 1) * 1024],
-            kv_buf[z].reshape(1024, 256)[:, 128:256],
-            preferred_element_type=F32,
+            weights[:, z * 1024 : (z + 1) * 1024], v_buf[z].reshape(1024, 128), preferred_element_type=F32
         )
-    mixed = (accum / total).astype(BF16)
-    feat.fill(mixed, co_buf)
-    feat.x1()
+    mixed = (accum / total).reshape(4, 4, 8, 128)
+    for x in range(4):
+        mix_send[x] = mixed[:, x].reshape(32, 128).astype(BF16)
+    for j in (1, 3, 2):
+        heads.copy(j, mix_send.at[at.xs(j)], mix_recv.at[at.x]).start()
+    mix_recv[at.x] = mix_send[at.x]
+    up.middle()
+    co_x.settle()
+    for j in (1, 3, 2):
+        heads.copy(j, mix_send.at[at.xs(j)], mix_recv.at[at.xs(-j)]).wait_recv()
+    mixed = jnp.concatenate([mix_recv[x] for x in range(4)], axis=1)
+    for n in range(4):
+        low, high = (
+            times_transposed(
+                mixed, jnp.concatenate([row_block(co_buf.at[x], m) for x in range(4)], axis=1)
+            ).reshape(4, 8, 384)
+            for m in (n, n + 4)
+        )
+        both = jnp.concatenate([low, high], axis=1)
+        feat32[:, :, n * 384 : (n + 1) * 384] = both
+        feat16[:, :, n * 384 : (n + 1) * 384] = both.astype(BF16)
+    for j in (2, 1, 3):
+        feats.copy(j, feat16.at[at.ws(j)], feat_recv.at[j - 1]).start()
+    down.middle()
     up.relay()
-    down.middle()
-    feat.x2()
-    feat.z1()
+    down.relay()
     up.finish()
-    down.relay()
-    feat.z2()
     down.finish()
-    hidden_grad[...] = jnp.dot(cotangent[...], down_buf[...].reshape(D, 384), preferred_element_type=F32)
-    summed = own_rows(base_hidden, at.tensor) + feat.done()
+    feat = feat32[at.w]
+    for j in (1, 3, 2):
+        feats.copy(j, feat16.at[at.ws(j)], feat_recv.at[j - 1]).wait_recv()
+        feat = feat + feat_recv[j - 1].astype(F32)
+    summed = own_rows(own_base[...], at.tensor) + jnp.concatenate([feat[0:8], feat[8:16]], axis=1)
     nhat, rstd = norm_rows(summed)
-    spread_buf[at.p, at.q, at.u, at.v] = jnp.concatenate([nhat[:, :HALF], nhat[:, HALF:]], axis=0).astype(BF16)
-    for level in range(5):
-        spread.step(level)
+    spread_buf[at.w, at.x] = jnp.concatenate([nhat[:, :HALF], nhat[:, HALF:]], axis=0).astype(BF16)
+    spread.start()
+    up.settle()
+    down.settle()
+    hidden_grad[...] = jnp.dot(own_cot[...], down_buf[...].reshape(D, 384), preferred_element_type=F32)
+    spread.finish()
     for k in range(8):
-        pair = []
-        for t in (2 * k, 2 * k + 1):
-            (u, v), (p, q) = gray(t // 4), gray(t % 4)
-            pair.append(spread_buf[p, q, u, v].astype(F32))
+        pair = [spread_buf[t // 4, t % 4].astype(F32) for t in (2 * k, 2 * k + 1)]
         for h in range(2):
             normed[k * 16 : (k + 1) * 16, h * HALF : (h + 1) * HALF] = jnp.concatenate(
                 [block[h * 8 : (h + 1) * 8] for block in pair], axis=0
@@ -390,13 +514,16 @@
     grad.z2()
     base_out[...] = summed + added.done()
     normed_grad = grad.done()
-    feat_grad[...] = own_rows(cotangent, at.tensor) + rstd * (
+    feat_grad[...] = own_rows(row_pair(own_cot, at.tensor)[...], at.tensor) + rstd * (
         normed_grad
         - jnp.mean(normed_grad, axis=-1, keepdims=True)
         - nhat * jnp.mean(normed_grad * nhat, axis=-1, keepdims=True)
     )
-    for each in (wp, kv, co, up, down, feat, added, grad, spread):
+    for each in (wq, wk, wv, ks, vs, co, up, down, co_x, spread, added, grad):
         each.drain()
+    for j in (1, 2, 3):
+        heads.copy(j, mix_send.at[at.xs(j)], mix_recv.at[at.x]).wait_send()
+        feats.copy(j, feat16.at[at.ws(j)], feat_recv.at[j - 1]).wait_send()
 
 
 def body(*args):
@@ -407,38 +534,53 @@
     out = pl.pallas_call(
         kernel,
         out_shape=[jax.ShapeDtypeStruct((8, D), F32)] * 2,
-        in_specs=[vmem] * 9,
+        in_specs=[pl.BlockSpec(memory_space=pltpu.HBM)] * 9,
         out_specs=[vmem] * 2,
         scratch_shapes=[
-            pltpu.VMEM((4, 8, 96, 384), BF16),
-            pltpu.VMEM((4, 8, 128, 256), BF16),
-            pltpu.VMEM((4, 8, 96, 128), BF16),
-            pltpu.VMEM((4, 8, 96, 384), BF16),
-            pltpu.VMEM((4, 8, 96, 384), BF16),
+            pltpu.VMEM((3, 4, 4, 2, 96, 128), BF16),
+            pltpu.VMEM((4, 4, 2, 128, 128), BF16),
+            pltpu.VMEM((4, 4, 2, 128, 128), BF16),
+            pltpu.VMEM((4, 4, 4, 2, 96, 128), BF16),
+            pltpu.VMEM((4, 4, 2, 96, 384), BF16),
+            pltpu.VMEM((4, 4, 2, 96, 384), BF16),
+            pltpu.VMEM((128, D), BF16),
+            pltpu.VMEM((2, 1, 128), F32),
+            pltpu.VMEM((16, D), BF16),
+            pltpu.VMEM((128, D), BF16),
             pltpu.VMEM((128, D), BF16),
             pltpu.VMEM((128, 4096), F32),
             pltpu.VMEM((128, 4096), BF16),
-            pltpu.VMEM((2, 2, 2, 2, 16, HALF), BF16),
+            pltpu.VMEM((4, 32, 128), BF16),
+            pltpu.VMEM((4, 32, 128), BF16),
+            pltpu.VMEM((4, 16, HALF), F32),
+            pltpu.VMEM((4, 16, HALF), BF16),
+            pltpu.VMEM((3, 16, HALF), BF16),
+            pltpu.VMEM((4, 4, 16, HALF), BF16),
             pltpu.VMEM((128, D), BF16),
             pltpu.VMEM((128, 384), F32),
-            pltpu.VMEM((3, 2, 2, 2, 2, 16, HALF), BF16),
-            pltpu.VMEM((3, 2, 2, 2, 2, 16, LANES), BF16),
-            pltpu.VMEM((3, 2, 2, 2, 16, LANES), BF16),
-            pltpu.VMEM((3, 2, 2, 2, 16, LANES), BF16),
-            pltpu.VMEM((3, 2, 2, 2, 16, LANES), F32),
-            pltpu.VMEM((3, 2, 2, 2, 16, LANES), BF16),
-            pltpu.VMEM((3, 2, 2, 16, LANES), BF16),
-            pltpu.VMEM((3, 2, 16, LANES), BF16),
-            pltpu.VMEM((3, 2, 16, LANES), BF16),
-            pltpu.SemaphoreType.DMA((5, 4)),
-            pltpu.SemaphoreType.DMA((5, 19)),
-            pltpu.SemaphoreType.DMA((3, 8)),
-            pltpu.SemaphoreType.DMA((3, 8)),
-            pltpu.SemaphoreType.DMA((8,)),
-            pltpu.SemaphoreType.DMA((8,)),
+            pltpu.VMEM((2, 2, 2, 2, 2, 16, HALF), BF16),
+            pltpu.VMEM((2, 2, 2, 2, 2, 16, LANES), BF16),
+            pltpu.VMEM((2, 2, 2, 2, 16, LANES), BF16),
+            pltpu.VMEM((2, 2, 2, 2, 16, LANES), BF16),
+            pltpu.VMEM((2, 2, 2, 2, 16, LANES), F32),
+            pltpu.VMEM((2, 2, 2, 2, 16, LANES), BF16),
+            pltpu.VMEM((2, 2, 2, 16, LANES), BF16),
+            pltpu.VMEM((2, 2, 16, LANES), BF16),
+            pltpu.VMEM((2, 2, 16, LANES), BF16),
+            pltpu.SemaphoreType.DMA((11,)),
+            pltpu.SemaphoreType.DMA((8, 4)),
+            pltpu.SemaphoreType.DMA((8, 19)),
+            pltpu.SemaphoreType.DMA((2,)),
+            pltpu.SemaphoreType.DMA((15,)),
+            pltpu.SemaphoreType.DMA((2, 3)),
+            pltpu.SemaphoreType.DMA((2, 3)),
+            pltpu.SemaphoreType.DMA((2, 8)),
+            pltpu.SemaphoreType.DMA((2, 8)),
+            pltpu.SemaphoreType.DMA((2,)),
+            pltpu.SemaphoreType.DMA((15,)),
         ],
         compiler_params=pltpu.CompilerParams(
-            collective_id=0, has_side_effects=True, vmem_limit_bytes=50 * 1024 * 1024
+            collective_id=0, has_side_effects=True, vmem_limit_bytes=64000 * 1024
         ),
     )(*args)
     return tuple(each.astype(BF16) for each in out)

time: 137 us -> 119 us (0.87)
  the two profiles are of different devices: /device:TPU:32 before, /device:TPU:28 now
where the time goes in v2:
time: 119 us
  Pallas kernels  116 us (97%)
  other arithmetic  2.18 us (2%)
    pallas_call x1, Pallas kernels, body(): pl.pallas_call(kernel, out_shape=[jax.ShapeDtypeStruct((8, D), F32)] * 2,...  116 us

profile of v2, /device:TPU:28, one launch (start us, length us, event | category | flops | bytes accessed | tf_op | source)
XLA Modules:
  0.0 119.1 jit_solution(13151565492032148671)
XLA Ops:
  0.6 116.3 %shard_map.104 = (f32[8,3072]{1,0:T(8,128)}, f32[8,3072]{1,0:T(8,128)}) custom-call(bf16[128,3072]{1,0:T(8,128)(2,1)} %control_in.1, bf16[3,96,128]{2,1,0:T(8,128)(2,1)} %control_project.1, bf16[96,128]{1,0:T(8,128)(2,1)} %control_output.1, f32[1,128]{1,0:T(1,128)} %bitcast.2, f32[1,128]{1,0:T(1,128)} %bitcast.3, bf16[128,3072]{1,0:T(8,128)(2,1)} %base_hidden.1, ...), custom_call_target="tpu_custom_call" | custom-call | tf_op jit(solution)/shard_map/pallas_call | solution.py:534
  116.9 0.0 copy-start
  117.0 1.6 %convert_element_type.6 = bf16[8,3072]{1,0:T(8,128)(2,1)} convert(f32[8,3072]{1,0:T(8,128)} %get-tuple-element.4) | non-fusion elementwise | flops 24576 | bytes 147456 | tf_op jit(solution)/shard_map/convert_element_type | solution.py:586
  118.5 0.0 copy-done
  118.5 0.6 convert_element_type.7
Async XLA Ops:
  116.9 1.6 %copy-start = (f32[8,3072]{1,0:T(8,128)S(1)}, f32[8,3072]{1,0:T(8,128)}, u32[]{:S(2)}) copy-start(f32[8,3072]{1,0:T(8,128)} %get-tuple-element.5) | copy-start | bytes 294916

commit v3 on v2

v3 whole, which is shorter than its diff:
```python
import functools

import jax
import jax.numpy as jnp
from jax import lax
from jax.experimental import pallas as pl
from jax.experimental.pallas import tpu as pltpu
from jax.sharding import PartitionSpec as P

F32 = jnp.float32
BF16 = jnp.bfloat16
MESH = pl.DeviceIdType.MESH
D = 3072
HALF = D // 2


def norm_rows(values):
    center = values - jnp.mean(values, axis=-1, keepdims=True)
    spread = jnp.mean(center * center, axis=-1, keepdims=True)
    rstd = lax.rsqrt(spread + 1e-06)
    return (center * rstd, rstd)


def head_norm(values, gain):
    square_mean = jnp.mean(values * values, axis=-1, keepdims=True)
    return (values * lax.rsqrt(square_mean + 1e-06) * gain).astype(BF16)


def times_transposed(left, right):
    return lax.dot_general(left, right, (((1,), (1,)), ((), ())), preferred_element_type=F32)


class Place:
    def __init__(self):
        dp, tensor = lax.axis_index("dp"), lax.axis_index("tensor")
        self.dp, self.tensor = dp, tensor
        self.z, self.y, self.c = dp // 8, lax.rem(dp // 2, 4), lax.rem(dp, 2)
        self.w, self.x = tensor // 4, lax.rem(tensor, 4)
        self.sibling = self.at(self.z, self.y, 1 - self.c)

    def at(self, z, y, c):
        return (z * 8 + y * 2 + c, self.tensor)

    def zs(self, j):
        return lax.rem(self.z + (j + 4), 4)

    def ys(self, j):
        return lax.rem(self.y + (j + 4), 4)

    def xs(self, j):
        return lax.rem(self.x + (j + 4), 4)

    def ws(self, j):
        return lax.rem(self.w + (j + 4), 4)

    def tensor_at(self, w, x):
        return (self.dp, w * 4 + x)

    def partners(self):
        return (
            self.z_peers()
            + self.y_peers()
            + [self.sibling]
            + self.x_peers()
            + self.w_peers()
        )

    def z_peers(self):
        return [self.at(self.zs(j), self.y, self.c) for j in (1, 2, 3)]

    def y_peers(self):
        return [self.at(self.z, self.ys(j), self.c) for j in (1, 2, 3)]

    def x_peers(self):
        return [self.tensor_at(self.w, self.xs(j)) for j in (1, 2, 3)]

    def w_peers(self):
        return [self.tensor_at(self.ws(j), self.x) for j in (1, 2, 3)]


def remote(src, dst, send, recv, device):
    return pltpu.make_async_remote_copy(
        src_ref=src, dst_ref=dst, send_sem=send, recv_sem=recv, device_id=device, device_id_type=MESH
    )


class Gather:
    def __init__(self, at, buf, send, recv):
        self.at, self.buf, self.send, self.recv = at, buf, send, recv

    def slot(self, z, y, c):
        return self.buf.at[z, y, c]

    def line(self, y, c):
        return self.buf.at[:, y, c]

    def copy(self, ref, group, sem, device):
        return remote(ref, ref, self.send.at[group], self.recv.at[sem], device)

    def wait(self, ref, sem):
        self.copy(ref, 0, sem, self.at.sibling).wait_recv()

    def both_ways(self, j):
        at = self.at
        ref = self.slot(at.zs(-j), at.y, at.c)
        self.copy(ref, 1, 3 + j, at.at(at.z, at.ys(1), at.c)).start()
        self.copy(ref, 1, 7 + j, at.at(at.z, at.ys(-1), at.c)).start()

    def start(self):
        at = self.at
        for j in (1, 3, 2):
            self.copy(self.slot(at.z, at.y, at.c), 0, j - 1, at.at(at.zs(j), at.y, at.c)).start()

    def middle(self, own=True):
        at = self.at
        if own:
            self.both_ways(0)
        for j in (1, 3, 2):
            self.wait(self.slot(at.zs(-j), at.y, at.c), j - 1)
            self.both_ways(j)
        self.copy(self.line(at.y, at.c), 3, 15, at.sibling).start()

    def relay(self):
        at = self.at
        for j in (0, 1, 3, 2):
            below, above = self.slot(at.zs(-j), at.ys(-1), at.c), self.slot(at.zs(-j), at.ys(1), at.c)
            self.wait(below, 3 + j)
            if j in (0, 3):
                self.copy(below, 2, 11 + j, at.at(at.z, at.ys(1), at.c)).start()
            self.wait(above, 7 + j)
            if j in (1, 2):
                self.copy(above, 2, 11 + j, at.at(at.z, at.ys(-1), at.c)).start()
        self.copy(self.line(at.ys(-1), at.c), 3, 16, at.sibling).start()
        self.copy(self.line(at.ys(1), at.c), 3, 17, at.sibling).start()

    def finish(self):
        at = self.at
        for j in (0, 1, 3, 2):
            self.wait(self.slot(at.zs(-j), at.ys(2), at.c), 11 + j)
        self.copy(self.line(at.ys(2), at.c), 3, 18, at.sibling).start()

    def settle(self):
        at = self.at
        for sem, step in ((15, 0), (16, -1), (17, 1), (18, 2)):
            self.wait(self.line(at.ys(step), 1 - at.c), sem)

    def drain(self):
        buf = self.buf
        for group, ref in enumerate((buf.at[0:3, 0, 0], buf.at[:, 0], buf.at[:, 0, 0], buf.at[:, :, 0])):
            self.copy(ref, group, 0, self.at.sibling).wait_send()


class Across:
    def __init__(self, at, buf, send, recv):
        self.at, self.buf, self.send, self.recv = at, buf, send, recv

    def line(self, x, step):
        return self.buf.at[x, :, self.at.ys(step), self.at.c]

    def copy(self, ref, group, sem, device):
        return remote(ref, ref, self.send.at[group], self.recv.at[sem], device)

    def start(self, *steps):
        at = self.at
        for step in steps:
            for i in (1, 3, 2):
                self.copy(self.line(at.x, step), 0, (step + 1) * 3 + i - 1, at.tensor_at(at.w, at.xs(i))).start()

    def swap(self):
        at = self.at
        for i in (1, 3, 2):
            for step in (0, -1, 1, 2):
                self.copy(self.line(at.xs(-i), step), 0, (step + 1) * 3 + i - 1, at.sibling).wait_recv()
            self.copy(self.buf.at[at.xs(-i), :, :, at.c], 1, 12 + i - 1, at.sibling).start()

    def settle(self):
        at = self.at
        for i in (1, 3, 2):
            self.copy(self.buf.at[at.xs(-i), :, :, 1 - at.c], 1, 12 + i - 1, at.sibling).wait_recv()

    def drain(self):
        for group in range(2):
            self.copy(self.buf.at[0:3, :, :, 0], group, 0, self.at.sibling).wait_send()


class Scatter:
    def __init__(self, at, part, from_x, total, from_w, x_send, x_recv, w_send, w_recv):
        self.at, self.part, self.from_x, self.total, self.from_w = at, part, from_x, total, from_w
        self.x_send, self.x_recv, self.w_send, self.w_recv = x_send, x_recv, w_send, w_recv

    def x_copy(self, j, i):
        at = self.at
        return remote(
            self.part.at[j, at.xs(i)], self.from_x.at[j, i - 1], self.x_send, self.x_recv.at[3 * j + i - 1],
            at.tensor_at(at.w, at.xs(i)),
        )

    def w_copy(self, j):
        at = self.at
        return remote(
            self.total.at[j - 1], self.from_w.at[j - 1], self.w_send, self.w_recv.at[j - 1],
            at.tensor_at(at.ws(-j), at.x),
        )

    def fill(self, groups, left, matrix):
        for n in range(4):
            low, high = (
                times_transposed(left, row_block(matrix, m)).reshape(4 * len(groups), 8, 384) for m in (n, n + 4)
            )
            both = jnp.concatenate([low, high], axis=1).astype(BF16)
            for k, j in enumerate(groups):
                for x in range(4):
                    self.part[j, x, :, n * 384 : (n + 1) * 384] = both[4 * k + x]
        for j in groups:
            for i in (1, 3, 2):
                self.x_copy(j, i).start()

    def sum_x(self, j):
        total = self.part[j, self.at.x].astype(F32)
        for i in (1, 3, 2):
            self.x_copy(j, i).wait_recv()
            total = total + self.from_x[j, i - 1].astype(F32)
        return total

    def pass_on(self, j):
        self.total[j - 1] = self.sum_x(j).astype(BF16)
        self.w_copy(j).start()

    def done(self):
        total = self.sum_x(0)
        for j in (1, 3, 2):
            self.w_copy(j).wait_recv()
            total = total + self.from_w[j - 1].astype(F32)
        return jnp.concatenate([total[0:8], total[8:16]], axis=1)

    def drain(self):
        at = self.at
        whole = self.part.at[0:3]
        remote(whole, whole, self.x_send, self.x_recv.at[0], at.sibling).wait_send()
        remote(self.total, self.total, self.w_send, self.w_recv.at[0], at.sibling).wait_send()


class Direct:
    def __init__(self, send, recv, peers):
        self.send, self.recv, self.peers = send, recv, peers

    def copy(self, j, src, dst):
        return remote(src, dst, self.send.at[j - 1], self.recv.at[j - 1], self.peers[j - 1])


class Lines:
    def __init__(self, at, buf, send, recv):
        self.at, self.buf, self.send, self.recv = at, buf, send, recv

    def copy(self, i, other=False):
        at = self.at
        ref = self.buf.at[at.ys(-i), 1 - at.c if other else at.c]
        return remote(ref, ref, self.send.at[3 + i], self.recv.at[3 + i], at.sibling)

    def along_y(self, i):
        at = self.at
        ref = self.buf.at[at.y, at.c]
        return remote(ref, ref, self.send.at[i - 1], self.recv.at[i - 1], at.y_peers()[i - 1])

    def start(self):
        for i in (2, 1, 3):
            self.along_y(i).start()
        self.copy(0).start()

    def middle(self):
        at = self.at
        for i in (1, 3, 2):
            ref = self.buf.at[at.ys(-i), at.c]
            remote(ref, ref, self.send.at[i - 1], self.recv.at[i - 1], at.sibling).wait_recv()
            self.copy(i).start()

    def settle(self):
        for i in (0, 1, 3, 2):
            self.copy(i, True).wait_recv()

    def drain(self):
        for i in (1, 2, 3):
            self.along_y(i).wait_send()
        for i in range(4):
            self.copy(i).wait_send()


class Spread:
    def __init__(self, at, buf, send, recv):
        self.at, self.buf, self.send, self.recv = at, buf, send, recv

    def copy(self, ref, group, sem, device):
        return remote(ref, ref, self.send.at[group], self.recv.at[sem], device)

    def along_x(self, j):
        at = self.at
        for i in (1, 3, 2):
            self.copy(self.buf.at[at.ws(-j), at.x], 1, 3 + 3 * j + i - 1, at.tensor_at(at.w, at.xs(i))).start()

    def start(self):
        at = self.at
        for j in (1, 3, 2):
            self.copy(self.buf.at[at.w, at.x], 0, j - 1, at.tensor_at(at.ws(j), at.x)).start()
        self.along_x(0)

    def forward(self, j):
        at = self.at
        self.copy(self.buf.at[at.ws(-j), at.x], 0, j - 1, at.sibling).wait_recv()
        self.along_x(j)

    def settle(self, j):
        at = self.at
        for i in (1, 3, 2):
            self.copy(self.buf.at[at.ws(-j), at.xs(-i)], 1, 3 + 3 * j + i - 1, at.sibling).wait_recv()

    def drain(self):
        self.copy(self.buf.at[0:3, 0], 0, 0, self.at.sibling).wait_send()
        self.copy(self.buf.at[0:3], 1, 0, self.at.sibling).wait_send()


def row_block(matrix, n):
    y = 2 * (n % 2)
    return matrix[n // 2, y : y + 2].reshape(384, matrix.shape[-1])


def row_pair(ref, tensor):
    return ref.at[pl.ds(pl.multiple_of((tensor // 2) * 16, 16), 16), :]


def own_rows(pair, tensor):
    pair = pair.astype(F32)
    return jnp.where(lax.rem(tensor, 2) == 0, pair[0:8], pair[8:16])


def kernel(
    control_in, control_project, control_output, query_gain, key_gain, base_hidden, base_up, base_down, cotangent,
    base_out, feat_grad,
    w_buf, kv_buf, q_buf, co_buf, up_buf, down_buf, own_in, own_gain, own_base, own_cot,
    normed_in, scores, stat, stat_back, mix32, mix16, mix_back, mix_send, mix_recv, feat32, feat16, feat_recv, spread_buf, normed, hidden_grad,
    part, from_x, total, from_w,
    local_sem, gather_send, gather_recv, kv_send, kv_recv, across_send, across_recv, direct_send, direct_recv,
    x_send, x_recv, w_send, w_recv, spread_send, spread_recv,
):
    at = Place()
    barrier = pltpu.get_barrier_semaphore()
    partners = at.partners()
    for device in partners:
        pl.semaphore_signal(barrier, inc=1, device_id=device, device_id_type=MESH)

    project, co, up, down = (
        Gather(at, buf, gather_send.at[i], gather_recv.at[i])
        for i, buf in enumerate((w_buf, co_buf.at[at.x], up_buf, down_buf))
    )
    kv = Lines(at, kv_buf, kv_send, kv_recv)
    ask = Direct(direct_send.at[2], direct_recv.at[2], at.z_peers())
    answer = Direct(direct_send.at[3], direct_recv.at[3], at.z_peers())
    answer_stat = Direct(direct_send.at[4], direct_recv.at[4], at.z_peers())
    co_x = Across(at, co_buf, across_send, across_recv)
    added, grad = (
        Scatter(at, *(ref.at[i] for ref in (part, from_x, total, from_w, x_send, x_recv, w_send, w_recv)))
        for i in range(2)
    )
    spread = Spread(at, spread_buf, spread_send, spread_recv)
    heads = Direct(direct_send.at[0], direct_recv.at[0], at.x_peers())
    feats = Direct(direct_send.at[1], direct_recv.at[1], at.w_peers())

    def own(gather):
        return gather.slot(at.z, at.y, at.c)

    loads = [
        pltpu.make_async_copy(src, dst, local_sem.at[i])
        for i, (src, dst) in enumerate(
            (
                (control_project.at[0], own(project).at[:, 0:128]),
                (control_project.at[1], own(project).at[:, 128:256]),
                (control_project.at[2], own(project).at[:, 256:384]),
                (control_in, own_in),
                (control_output, own(co)),
                (query_gain, own_gain.at[0]),
                (key_gain, own_gain.at[1]),
                (base_up, own(up)),
                (base_down, own(down)),
                (row_pair(base_hidden, at.tensor), own_base),
                (cotangent, own_cot),
            )
        )
    ]
    for load in loads:
        load.start()
    pl.semaphore_wait(barrier, len(partners))

    for load in loads[0:3]:
        load.wait()
    project.start()
    project.both_ways(0)
    loads[3].wait()
    normed_in[...] = norm_rows(own_in[...].astype(F32))[0].astype(BF16)
    project.middle(False)
    for load in loads[4:]:
        load.wait()
    co.start()
    up.start()
    down.start()
    project.relay()
    project.finish()
    co.middle()
    co_x.start(0)
    project.settle()
    projected = jnp.dot(normed_in[...], w_buf[...].reshape(D, 384), preferred_element_type=F32)
    kv_buf[at.y, at.c, :, 0:128] = head_norm(projected[:, 128:256], own_gain[1])
    kv_buf[at.y, at.c, :, 128:256] = projected[:, 256:384].astype(BF16)
    kv.start()
    q_buf[at.z] = head_norm(projected[:, 0:128], own_gain[0])
    for j in (2, 1, 3):
        ask.copy(j, q_buf.at[at.z], q_buf.at[at.z]).start()
    co.relay()
    co_x.start(-1, 1)
    kv.middle()
    co.finish()
    co_x.start(2)
    up.middle()
    for j in (1, 3, 2):
        ask.copy(j, q_buf.at[at.z], q_buf.at[at.zs(-j)]).wait_recv()
    kv.settle()
    asked = q_buf[...].reshape(512, 128)
    for y in range(4):
        block = kv_buf[y].reshape(256, 256)[:, 0:128]
        scores[y * 256 : (y + 1) * 256, :] = times_transposed(block, asked) * (1.0 / 128**0.5)
    values = kv_buf[...].reshape(1024, 256)[:, 128:256]
    for z in range(4):
        block = scores[:, z * 128 : (z + 1) * 128]
        top = jnp.max(block, axis=0, keepdims=True)
        expo = jnp.exp(block - top)
        sums = jnp.sum(expo, axis=0, keepdims=True)
        stat[z] = jnp.concatenate([top, sums, jnp.zeros((6, 128), F32)], axis=0)
        accum = lax.dot_general(
            values, expo.astype(BF16), (((0,), (0,)), ((), ())), preferred_element_type=F32
        )
        mix32[z] = accum
        mix16[z] = accum.astype(BF16)
    for j in (2, 1, 3):
        answer.copy(j, mix16.at[at.zs(j)], mix_back.at[j - 1]).start()
        answer_stat.copy(j, stat.at[at.zs(j)], stat_back.at[j - 1]).start()
    co.settle()
    co_x.swap()
    down.middle()
    accums, stats = [mix32[at.z]], [stat[at.z]]
    for j in (1, 3, 2):
        answer.copy(j, mix16.at[at.zs(j)], mix_back.at[j - 1]).wait_recv()
        answer_stat.copy(j, stat.at[at.zs(j)], stat_back.at[j - 1]).wait_recv()
        accums.append(mix_back[j - 1].astype(F32))
        stats.append(stat_back[j - 1])
    top = functools.reduce(jnp.maximum, [each[0:1] for each in stats])
    shares = [jnp.exp(each[0:1] - top) for each in stats]
    row_sum = sum(share * each[1:2] for share, each in zip(shares, stats))
    mixed = sum(share * each for share, each in zip(shares, accums)) / row_sum
    mixed = jnp.transpose(mixed).reshape(4, 4, 8, 128)
    for x in range(4):
        mix_send[x] = mixed[:, x].reshape(32, 128).astype(BF16)
    for j in (1, 3, 2):
        heads.copy(j, mix_send.at[at.xs(j)], mix_recv.at[at.x]).start()
    mix_recv[at.x] = mix_send[at.x]
    up.relay()
    co_x.settle()
    for j in (1, 3, 2):
        heads.copy(j, mix_send.at[at.xs(j)], mix_recv.at[at.xs(-j)]).wait_recv()
    mixed = jnp.concatenate([mix_recv[x] for x in range(4)], axis=1)
    for n in range(4):
        low, high = (
            times_transposed(
                mixed, jnp.concatenate([row_block(co_buf.at[x], m) for x in range(4)], axis=1)
            ).reshape(4, 8, 384)
            for m in (n, n + 4)
        )
        both = jnp.concatenate([low, high], axis=1)
        feat32[:, :, n * 384 : (n + 1) * 384] = both
        feat16[:, :, n * 384 : (n + 1) * 384] = both.astype(BF16)
    for j in (2, 1, 3):
        feats.copy(j, feat16.at[at.ws(j)], feat_recv.at[j - 1]).start()
    down.relay()
    up.finish()
    down.finish()
    feat = feat32[at.w]
    for j in (1, 3, 2):
        feats.copy(j, feat16.at[at.ws(j)], feat_recv.at[j - 1]).wait_recv()
        feat = feat + feat_recv[j - 1].astype(F32)
    summed = own_rows(own_base[...], at.tensor) + jnp.concatenate([feat[0:8], feat[8:16]], axis=1)
    nhat, rstd = norm_rows(summed)
    spread_buf[at.w, at.x] = jnp.concatenate([nhat[:, :HALF], nhat[:, HALF:]], axis=0).astype(BF16)
    spread.start()
    up.settle()
    down.settle()
    hidden_grad[...] = jnp.dot(
        own_cot[...], down_buf[...].reshape(D, 384), preferred_element_type=F32
    ).reshape(4, 32, 384)

    def mlp(*groups):
        for j in groups:
            spread.settle(j)
            w = at.ws(-j)
            blocks = [spread_buf[w, x].astype(F32) for x in range(4)]
            for k in (0, 2):
                for h in range(2):
                    normed[j, k * 8 : k * 8 + 16, h * HALF : (h + 1) * HALF] = jnp.concatenate(
                        [block[h * 8 : (h + 1) * 8] for block in blocks[k : k + 2]], axis=0
                    ).astype(BF16)
        pre = jnp.dot(
            jnp.concatenate([normed[j] for j in groups], axis=0), up_buf[...].reshape(D, 384), preferred_element_type=F32
        )
        tangent = jnp.tanh(0.7978845608028654 * (pre + 0.044715 * pre * pre * pre))
        hidden = (0.5 * pre * (1.0 + tangent)).astype(BF16)
        slope = 0.5 * (1.0 + tangent) + 0.5 * pre * (1.0 - tangent * tangent) * 0.7978845608028654 * (
            1.0 + 3.0 * 0.044715 * pre * pre
        )
        arriving = jnp.concatenate([hidden_grad[at.ws(-j)] for j in groups], axis=0)
        added.fill(groups, hidden, down_buf)
        grad.fill(groups, (arriving * slope).astype(BF16), up_buf)

    mlp(0)
    spread.forward(1)
    spread.forward(3)
    spread.forward(2)
    mlp(1, 3)
    mlp(2)
    for j in (1, 3, 2):
        added.pass_on(j)
        grad.pass_on(j)
    base_out[...] = summed + added.done()
    normed_grad = grad.done()
    feat_grad[...] = own_rows(row_pair(own_cot, at.tensor)[...], at.tensor) + rstd * (
        normed_grad
        - jnp.mean(normed_grad, axis=-1, keepdims=True)
        - nhat * jnp.mean(normed_grad * nhat, axis=-1, keepdims=True)
    )
    for each in (project, kv, co, up, down, co_x, spread, added, grad):
        each.drain()
    for j in (1, 2, 3):
        ask.copy(j, q_buf.at[at.z], q_buf.at[at.z]).wait_send()
        answer.copy(j, mix16.at[at.zs(j)], mix_back.at[j - 1]).wait_send()
        answer_stat.copy(j, stat.at[at.zs(j)], stat_back.at[j - 1]).wait_send()
        heads.copy(j, mix_send.at[at.xs(j)], mix_recv.at[at.x]).wait_send()
        feats.copy(j, feat16.at[at.ws(j)], feat_recv.at[j - 1]).wait_send()


def body(*args):
    args = list(args)
    args[3] = args[3].reshape(1, 128)
    args[4] = args[4].reshape(1, 128)
    vmem = pl.BlockSpec(memory_space=pltpu.VMEM)
    out = pl.pallas_call(
        kernel,
        out_shape=[jax.ShapeDtypeStruct((8, D), F32)] * 2,
        in_specs=[pl.BlockSpec(memory_space=pltpu.HBM)] * 9,
        out_specs=[vmem] * 2,
        scratch_shapes=[
            pltpu.VMEM((4, 4, 2, 96, 384), BF16),
            pltpu.VMEM((4, 2, 128, 256), BF16),
            pltpu.VMEM((4, 128, 128), BF16),
            pltpu.VMEM((4, 4, 4, 2, 96, 128), BF16),
            pltpu.VMEM((4, 4, 2, 96, 384), BF16),
            pltpu.VMEM((4, 4, 2, 96, 384), BF16),
            pltpu.VMEM((128, D), BF16),
            pltpu.VMEM((2, 1, 128), F32),
            pltpu.VMEM((16, D), BF16),
            pltpu.VMEM((128, D), BF16),
            pltpu.VMEM((128, D), BF16),
            pltpu.VMEM((1024, 512), F32),
            pltpu.VMEM((4, 8, 128), F32),
            pltpu.VMEM((3, 8, 128), F32),
            pltpu.VMEM((4, 128, 128), F32),
            pltpu.VMEM((4, 128, 128), BF16),
            pltpu.VMEM((3, 128, 128), BF16),
            pltpu.VMEM((4, 32, 128), BF16),
            pltpu.VMEM((4, 32, 128), BF16),
            pltpu.VMEM((4, 16, HALF), F32),
            pltpu.VMEM((4, 16, HALF), BF16),
            pltpu.VMEM((3, 16, HALF), BF16),
            pltpu.VMEM((4, 4, 16, HALF), BF16),
            pltpu.VMEM((4, 32, D), BF16),
            pltpu.VMEM((4, 32, 384), F32),
            pltpu.VMEM((2, 4, 4, 16, HALF), BF16),
            pltpu.VMEM((2, 4, 3, 16, HALF), BF16),
            pltpu.VMEM((2, 3, 16, HALF), BF16),
            pltpu.VMEM((2, 3, 16, HALF), BF16),
            pltpu.SemaphoreType.DMA((11,)),
            pltpu.SemaphoreType.DMA((4, 4)),
            pltpu.SemaphoreType.DMA((4, 19)),
            pltpu.SemaphoreType.DMA((7,)),
            pltpu.SemaphoreType.DMA((7,)),
            pltpu.SemaphoreType.DMA((2,)),
            pltpu.SemaphoreType.DMA((15,)),
            pltpu.SemaphoreType.DMA((5, 3)),
            pltpu.SemaphoreType.DMA((5, 3)),
            pltpu.SemaphoreType.DMA((2,)),
            pltpu.SemaphoreType.DMA((2, 12)),
            pltpu.SemaphoreType.DMA((2,)),
            pltpu.SemaphoreType.DMA((2, 3)),
            pltpu.SemaphoreType.DMA((2,)),
            pltpu.SemaphoreType.DMA((15,)),
        ],
        compiler_params=pltpu.CompilerParams(
            collective_id=0, has_side_effects=True, vmem_limit_bytes=64000 * 1024
        ),
    )(*args)
    return tuple(each.astype(BF16) for each in out)


def solution(mesh):
    placed = (
        P("dp", None),
        P(None, "dp", "tensor"),
        P("dp", "tensor"),
        P(),
        P(),
        P("dp", None),
        P("dp", "tensor"),
        P("dp", "tensor"),
        P("dp", None),
    )
    return jax.shard_map(
        body,
        mesh=mesh,
        in_specs=placed,
        out_specs=(P(("dp", "tensor"), None), P(("dp", "tensor"), None)),
        check_vma=False,
    )
```

time: 119 us -> 116 us (0.975)
  the two profiles are of different devices: /device:TPU:28 before, /device:TPU:6 now
where the time goes in v3:
time: 116 us
  Pallas kernels  113 us (97%)
  other arithmetic  2.18 us (2%)
    pallas_call x1, Pallas kernels, body(): pl.pallas_call(kernel, out_shape=[jax.ShapeDtypeStruct((8, D), F32)] * 2,...  113 us

profile of v3, /device:TPU:6, one launch (start us, length us, event | category | flops | bytes accessed | tf_op | source)
XLA Modules:
  0.0 116.0 jit_solution(13760233247995124582)
XLA Ops:
  0.6 113.2 %shard_map.104 = (f32[8,3072]{1,0:T(8,128)}, f32[8,3072]{1,0:T(8,128)}) custom-call(bf16[128,3072]{1,0:T(8,128)(2,1)} %control_in.1, bf16[3,96,128]{2,1,0:T(8,128)(2,1)} %control_project.1, bf16[96,128]{1,0:T(8,128)(2,1)} %control_output.1, f32[1,128]{1,0:T(1,128)} %bitcast.2, f32[1,128]{1,0:T(1,128)} %bitcast.3, bf16[128,3072]{1,0:T(8,128)(2,1)} %base_hidden.1, ...), custom_call_target="tpu_custom_call" | custom-call | tf_op jit(solution)/shard_map/pallas_call | solution.py:550
  113.8 0.0 copy-start
  113.8 1.6 %convert_element_type.6 = bf16[8,3072]{1,0:T(8,128)(2,1)} convert(f32[8,3072]{1,0:T(8,128)} %get-tuple-element.4) | non-fusion elementwise | flops 24576 | bytes 147456 | tf_op jit(solution)/shard_map/convert_element_type | solution.py:605
  115.4 0.0 copy-done
  115.4 0.6 convert_element_type.7
Async XLA Ops:
  113.8 1.6 %copy-start = (f32[8,3072]{1,0:T(8,128)S(1)}, f32[8,3072]{1,0:T(8,128)}, u32[]{:S(2)}) copy-start(f32[8,3072]{1,0:T(8,128)} %get-tuple-element.5) | copy-start | bytes 294916

commit v4 on v3

--- a/solution.py
+++ b/solution.py
@@ -200,6 +200,13 @@
         return remote(
             self.total.at[j - 1], self.from_w.at[j - 1], self.w_send, self.w_recv.at[j - 1],
             at.tensor_at(at.ws(-j), at.x),
+        )
+
+    def half_copy(self, h):
+        at, lanes = self.at, pl.ds(h * (HALF // 2), HALF // 2)
+        return remote(
+            self.total.at[1, :, lanes], self.from_w.at[1, :, lanes], self.w_send, self.w_recv.at[3 if h else 1],
+            at.tensor_at(at.ws(-1 if h else 1), at.x),
         )
 
     def fill(self, groups, left, matrix):
@@ -222,13 +229,24 @@
             total = total + self.from_x[j, i - 1].astype(F32)
         return total
 
-    def pass_on(self, j):
-        self.total[j - 1] = self.sum_x(j).astype(BF16)
+    def far(self):
+        self.total[1] = self.sum_x(2).astype(BF16)
+        for h in range(2):
+            self.half_copy(h).start()
+
+    def near(self, j):
+        h = 1 if j == 1 else 0
+        total = self.sum_x(j)
+        self.half_copy(h).wait_recv()
+        low, high = total[:, : HALF // 2], total[:, HALF // 2 :]
+        half = self.from_w[1, :, h * (HALF // 2) : (h + 1) * (HALF // 2)].astype(F32)
+        total = jnp.concatenate([low, high + half] if h else [low + half, high], axis=1)
+        self.total[j - 1] = total.astype(BF16)
         self.w_copy(j).start()
 
     def done(self):
         total = self.sum_x(0)
-        for j in (1, 3, 2):
+        for j in (1, 3):
             self.w_copy(j).wait_recv()
             total = total + self.from_w[j - 1].astype(F32)
         return jnp.concatenate([total[0:8], total[8:16]], axis=1)
@@ -299,13 +317,22 @@
 
     def start(self):
         at = self.at
-        for j in (1, 3, 2):
+        for j in (1, 3):
             self.copy(self.buf.at[at.w, at.x], 0, j - 1, at.tensor_at(at.ws(j), at.x)).start()
         self.along_x(0)
 
+    def half(self, j, h):
+        return self.buf.at[self.at.ws(-j), self.at.x, :, pl.ds(h * (HALF // 2), HALF // 2)]
+
     def forward(self, j):
         at = self.at
-        self.copy(self.buf.at[at.ws(-j), at.x], 0, j - 1, at.sibling).wait_recv()
+        if j == 2:
+            self.copy(self.half(2, 0), 0, 1, at.sibling).wait_recv()
+            self.copy(self.half(2, 1), 0, 15, at.sibling).wait_recv()
+        else:
+            self.copy(self.buf.at[at.ws(-j), at.x], 0, j - 1, at.sibling).wait_recv()
+            h = 0 if j == 1 else 1
+            self.copy(self.half(j, h), 0, 15 if h else 1, at.tensor_at(at.ws(j), at.x)).start()
         self.along_x(j)
 
     def settle(self, j):
@@ -399,12 +426,14 @@
     for load in loads[4:]:
         load.wait()
     co.start()
+    project.relay()
+    co.middle()
+    co_x.start(0)
     up.start()
     down.start()
-    project.relay()
     project.finish()
-    co.middle()
-    co_x.start(0)
+    co.relay()
+    co_x.start(-1, 1)
     project.settle()
     projected = jnp.dot(normed_in[...], w_buf[...].reshape(D, 384), preferred_element_type=F32)
     kv_buf[at.y, at.c, :, 0:128] = head_norm(projected[:, 128:256], own_gain[1])
@@ -413,8 +442,6 @@
     q_buf[at.z] = head_norm(projected[:, 0:128], own_gain[0])
     for j in (2, 1, 3):
         ask.copy(j, q_buf.at[at.z], q_buf.at[at.z]).start()
-    co.relay()
-    co_x.start(-1, 1)
     kv.middle()
     co.finish()
     co_x.start(2)
@@ -520,11 +547,13 @@
     spread.forward(1)
     spread.forward(3)
     spread.forward(2)
-    mlp(1, 3)
-    mlp(2)
-    for j in (1, 3, 2):
-        added.pass_on(j)
-        grad.pass_on(j)
+    mlp(2, 1, 3)
+    added.far()
+    grad.far()
+    for j in (1, 3):
+        added.near(j)
+    for j in (1, 3):
+        grad.near(j)
     base_out[...] = summed + added.done()
     normed_grad = grad.done()
     feat_grad[...] = own_rows(row_pair(own_cot, at.tensor)[...], at.tensor) + rstd * (
@@ -594,9 +623,9 @@
             pltpu.SemaphoreType.DMA((2,)),
             pltpu.SemaphoreType.DMA((2, 12)),
             pltpu.SemaphoreType.DMA((2,)),
-            pltpu.SemaphoreType.DMA((2, 3)),
+            pltpu.SemaphoreType.DMA((2, 4)),
             pltpu.SemaphoreType.DMA((2,)),
-            pltpu.SemaphoreType.DMA((15,)),
+            pltpu.SemaphoreType.DMA((16,)),
         ],
         compiler_params=pltpu.CompilerParams(
             collective_id=0, has_side_effects=True, vmem_limit_bytes=64000 * 1024

time: 116 us -> 111 us (0.957); the launches traced: 116 us -> 110 us
  Pallas kernels: 113 us -> 107 us
    pallas_call x1, Pallas kernels: 113 us -> 107 us  [body(): pl.pallas_call(kernel, out_shape=[jax.ShapeDtypeStruct((8, D), F32)] * 2,...]
where the time goes in v4:
time: 111 us; the launch traced here: 110 us
  Pallas kernels  107 us (96%)
  other arithmetic  2.18 us (2%)
    pallas_call x1, Pallas kernels, body(): pl.pallas_call(kernel, out_shape=[jax.ShapeDtypeStruct((8, D), F32)] * 2,...  107 us

profile of v4, /device:TPU:6, one launch (start us, length us, event | category | flops | bytes accessed | tf_op | source)
XLA Modules:
  0.0 109.6 jit_solution(10046762706341449121)
XLA Ops:
  0.6 106.8 %shard_map.104 = (f32[8,3072]{1,0:T(8,128)}, f32[8,3072]{1,0:T(8,128)}) custom-call(bf16[128,3072]{1,0:T(8,128)(2,1)} %control_in.1, bf16[3,96,128]{2,1,0:T(8,128)(2,1)} %control_project.1, bf16[96,128]{1,0:T(8,128)(2,1)} %control_output.1, f32[1,128]{1,0:T(1,128)} %bitcast.2, f32[1,128]{1,0:T(1,128)} %bitcast.3, bf16[128,3072]{1,0:T(8,128)(2,1)} %base_hidden.1, ...), custom_call_target="tpu_custom_call" | custom-call | tf_op jit(solution)/shard_map/pallas_call | solution.py:579
  107.4 0.0 copy-start
  107.4 1.6 %convert_element_type.6 = bf16[8,3072]{1,0:T(8,128)(2,1)} convert(f32[8,3072]{1,0:T(8,128)} %get-tuple-element.4) | non-fusion elementwise | flops 24576 | bytes 147456 | tf_op jit(solution)/shard_map/convert_element_type | solution.py:634
  109.0 0.0 copy-done
  109.0 0.6 convert_element_type.7
Async XLA Ops:
  107.4 1.6 %copy-start = (f32[8,3072]{1,0:T(8,128)S(1)}, f32[8,3072]{1,0:T(8,128)}, u32[]{:S(2)}) copy-start(f32[8,3072]{1,0:T(8,128)} %get-tuple-element.5) | copy-start | bytes 294916

commit v5 on v4

--- a/solution.py
+++ b/solution.py
@@ -547,7 +547,8 @@
     spread.forward(1)
     spread.forward(3)
     spread.forward(2)
-    mlp(2, 1, 3)
+    mlp(2)
+    mlp(1, 3)
     added.far()
     grad.far()
     for j in (1, 3):

time: 111 us -> 109 us (0.982)
  no operation moved by 1% of the time
where the time goes in v5:
time: 109 us
  Pallas kernels  106 us (97%)
  other arithmetic  2.18 us (2%)
    pallas_call x1, Pallas kernels, body(): pl.pallas_call(kernel, out_shape=[jax.ShapeDtypeStruct((8, D), F32)] * 2,...  106 us

profile of v5, /device:TPU:6, one launch (start us, length us, event | category | flops | bytes accessed | tf_op | source)
XLA Modules:
  0.0 108.7 jit_solution(4589814550818310229)
XLA Ops:
  0.6 105.9 %shard_map.104 = (f32[8,3072]{1,0:T(8,128)}, f32[8,3072]{1,0:T(8,128)}) custom-call(bf16[128,3072]{1,0:T(8,128)(2,1)} %control_in.1, bf16[3,96,128]{2,1,0:T(8,128)(2,1)} %control_project.1, bf16[96,128]{1,0:T(8,128)(2,1)} %control_output.1, f32[1,128]{1,0:T(1,128)} %bitcast.2, f32[1,128]{1,0:T(1,128)} %bitcast.3, bf16[128,3072]{1,0:T(8,128)(2,1)} %base_hidden.1, ...), custom_call_target="tpu_custom_call" | custom-call | tf_op jit(solution)/shard_map/pallas_call | solution.py:580
  106.5 0.0 copy-start
  106.5 1.6 %convert_element_type.6 = bf16[8,3072]{1,0:T(8,128)(2,1)} convert(f32[8,3072]{1,0:T(8,128)} %get-tuple-element.4) | non-fusion elementwise | flops 24576 | bytes 147456 | tf_op jit(solution)/shard_map/convert_element_type | solution.py:635
  108.1 0.0 copy-done
  108.1 0.6 convert_element_type.7
Async XLA Ops:
  106.5 1.6 %copy-start = (f32[8,3072]{1,0:T(8,128)S(1)}, f32[8,3072]{1,0:T(8,128)}, u32[]{:S(2)}) copy-start(f32[8,3072]{1,0:T(8,128)} %get-tuple-element.5) | copy-start | bytes 294916

commit v6 on v5

--- a/solution.py
+++ b/solution.py
@@ -515,6 +515,8 @@
     nhat, rstd = norm_rows(summed)
     spread_buf[at.w, at.x] = jnp.concatenate([nhat[:, :HALF], nhat[:, HALF:]], axis=0).astype(BF16)
     spread.start()
+    spread.forward(1)
+    spread.forward(3)
     up.settle()
     down.settle()
     hidden_grad[...] = jnp.dot(
@@ -543,10 +545,8 @@
         added.fill(groups, hidden, down_buf)
         grad.fill(groups, (arriving * slope).astype(BF16), up_buf)
 
+    spread.forward(2)
     mlp(0)
-    spread.forward(1)
-    spread.forward(3)
-    spread.forward(2)
     mlp(2)
     mlp(1, 3)
     added.far()

time: 109 us -> 108 us (level)
  Pallas kernels: 106 us -> 104 us
    pallas_call x1, Pallas kernels: 106 us -> 104 us  [body(): pl.pallas_call(kernel, out_shape=[jax.ShapeDtypeStruct((8, D), F32)] * 2,...]
where the time goes in v6:
time: 108 us; the launch traced here: 107 us
  Pallas kernels  104 us (96%)
  other arithmetic  2.18 us (2%)
    pallas_call x1, Pallas kernels, body(): pl.pallas_call(kernel, out_shape=[jax.ShapeDtypeStruct((8, D), F32)] * 2,...  104 us
    convert_element_type x2, other arithmetic, body(): return tuple((each.astype(BF16) for each in out))  2.18 us

profile of v6, /device:TPU:6, one launch (start us, length us, event | category | flops | bytes accessed | tf_op | source)
XLA Modules:
  0.0 106.7 jit_solution(16835863244842163950)
XLA Ops:
  0.6 103.8 %shard_map.104 = (f32[8,3072]{1,0:T(8,128)}, f32[8,3072]{1,0:T(8,128)}) custom-call(bf16[128,3072]{1,0:T(8,128)(2,1)} %control_in.1, bf16[3,96,128]{2,1,0:T(8,128)(2,1)} %control_project.1, bf16[96,128]{1,0:T(8,128)(2,1)} %control_output.1, f32[1,128]{1,0:T(1,128)} %bitcast.2, f32[1,128]{1,0:T(1,128)} %bitcast.3, bf16[128,3072]{1,0:T(8,128)(2,1)} %base_hidden.1, ...), custom_call_target="tpu_custom_call" | custom-call | tf_op jit(solution)/shard_map/pallas_call | solution.py:580
  104.5 0.0 copy-start
  104.5 1.6 %convert_element_type.6 = bf16[8,3072]{1,0:T(8,128)(2,1)} convert(f32[8,3072]{1,0:T(8,128)} %get-tuple-element.4) | non-fusion elementwise | flops 24576 | bytes 147456 | tf_op jit(solution)/shard_map/convert_element_type | solution.py:635
  106.0 0.0 copy-done
  106.0 0.6 convert_element_type.7
Async XLA Ops:
  104.5 1.6 %copy-start = (f32[8,3072]{1,0:T(8,128)S(1)}, f32[8,3072]{1,0:T(8,128)}, u32[]{:S(2)}) copy-start(f32[8,3072]{1,0:T(8,128)} %get-tuple-element.5) | copy-start | bytes 294916
